TPU v7x, 32 devices: a whole 2x2x4 slice. The times are simulated.
32 devices in a mesh: dp: 2 (over y), seq: 16 (over z, x, core).
Axes of the slice: x: 2, y: 2, z: 4, core: 2. Of those that a mesh axis runs over, the one named last changes fastest.
Arguments:
- queries: bfloat16 [2, 1024, 8192], P('dp', 'seq'), may hold values from -8 to 8
- keys: bfloat16 [2, 1024, 1024], P('dp', 'seq'), may hold values from -8 to 8
- values: bfloat16 [2, 1024, 1024], P('dp', 'seq'), may hold values from -6 to 6
- doc_lengths: int32 [2, 129], replicated, may hold values from 0 to 512, as said below
Outputs:
- attended: bfloat16 [2, 1024, 8192], P('dp', 'seq')
Inputs may be any that keep to these rules, and one draw needn't show every extreme that they name: `doc_lengths`: each row sums to 1024; zeros stand only after the last document; the first document of every row has 32 tokens and the second exactly 512.
All inputs are finite; a program needn't handle non-finite values.
Results may differ from a plain program's by a relative error of at most 0.0045.
Values may be sent and summed in bfloat16 or wider, within the bound.
No kernel may reach another device: no remote copies, remote signals or barrier semaphores. Data moves between devices by JAX's collectives and lax.ppermute only.
A program may use at most 64 MiB of HBM per device.

v0:
```python
import math

import jax
import jax.numpy as jnp
from jax import lax
from jax.sharding import PartitionSpec as P

QH = 64
KVH = 8
HD = 128
GROUP = 8


def shifted(block, axis, distance):
    devices = range(lax.axis_size(axis))
    route = [(i - distance, i) for i in devices if i - distance in devices]
    return lax.ppermute(block, axis, route)


def doc_starts(lengths_row, positions):
    doc_ends = jnp.cumsum(lengths_row)
    return jnp.max(jnp.where(doc_ends[None, :] <= positions[:, None], doc_ends, 0), axis=1)


def per_device(queries, keys, values, doc_lengths):
    tokens_here = queries.shape[1]
    seq_count = lax.axis_size("seq")
    score_scale = 1.0 / math.sqrt(HD)
    lengths_row = lax.dynamic_index_in_dim(doc_lengths, lax.axis_index("dp"), 0, keepdims=False)
    longest_doc = tokens_here * seq_count // 2
    reach = longest_doc // tokens_here
    local_keys = keys[0].reshape(tokens_here, KVH, HD)
    local_values = values[0].reshape(tokens_here, KVH, HD)
    key_store = jnp.zeros((reach + 1, tokens_here, KVH, HD), jnp.bfloat16).at[reach].set(local_keys)
    value_store = (
        jnp.zeros((reach + 1, tokens_here, KVH, HD), jnp.bfloat16).at[reach].set(local_values)
    )

    def receive_step(index, carry):
        moving_keys, moving_values, stored_keys, stored_values = carry
        moving_keys, moving_values = shifted((moving_keys, moving_values), "seq", 1)
        slot = reach - 1 - index
        stored_keys = lax.dynamic_update_index_in_dim(stored_keys, moving_keys, slot, 0)
        stored_values = lax.dynamic_update_index_in_dim(stored_values, moving_values, slot, 0)
        return (moving_keys, moving_values, stored_keys, stored_values)

    carried = lax.fori_loop(
        0, reach, receive_step, (local_keys, local_values, key_store, value_store)
    )
    key_store, value_store = (carried[2], carried[3])
    first_position = lax.axis_index("seq") * tokens_here
    base_position = first_position - reach * tokens_here
    grouped = queries[0].reshape(tokens_here, KVH, GROUP, HD)
    positions = first_position + jnp.arange(tokens_here, dtype=jnp.int32)
    starts = doc_starts(lengths_row, positions)
    first_slot = jnp.maximum((jnp.min(starts) - base_position) // tokens_here, 0)

    def tile(index):
        key_tile = lax.dynamic_index_in_dim(key_store, index, 0, keepdims=False)
        key_positions = (
            base_position + index * tokens_here + jnp.arange(tokens_here, dtype=jnp.int32)
        )
        allowed = (key_positions[None, :] >= starts[:, None]) & (
            key_positions[None, :] <= positions[:, None]
        )
        scores = (
            jnp.einsum("qkgd,tkd->kgqt", grouped, key_tile, preferred_element_type=jnp.float32)
            * score_scale
        )
        return (scores, allowed)

    def peak_step(index, peak):
        scores, allowed = tile(index)
        return jnp.maximum(peak, jnp.max(jnp.where(allowed[None, None], scores, -jnp.inf), axis=-1))

    peak = lax.fori_loop(
        first_slot, reach + 1, peak_step, jnp.full((KVH, GROUP, tokens_here), -jnp.inf, jnp.float32)
    )

    def sum_step(index, carry):
        total, summed = carry
        scores, allowed = tile(index)
        weights = jnp.where(allowed[None, None], jnp.exp(scores - peak[..., None]), 0.0).astype(
            jnp.bfloat16
        )
        value_tile = lax.dynamic_index_in_dim(value_store, index, 0, keepdims=False)
        total = total + jnp.sum(weights.astype(jnp.float32), axis=-1)
        summed = summed + jnp.einsum(
            "kgqt,tkd->qkgd", weights, value_tile, preferred_element_type=jnp.float32
        )
        return (total, summed)

    total, summed = lax.fori_loop(
        first_slot,
        reach + 1,
        sum_step,
        (
            jnp.zeros((KVH, GROUP, tokens_here), jnp.float32),
            jnp.zeros((tokens_here, KVH, GROUP, HD), jnp.float32),
        ),
    )
    result = summed / jnp.transpose(total, (2, 0, 1))[..., None]
    return result.astype(jnp.bfloat16).reshape(1, tokens_here, QH * HD)


def solution(mesh):
    placed = (P("dp", "seq", None), P("dp", "seq", None), P("dp", "seq", None), P())
    return jax.shard_map(
        per_device, mesh=mesh, in_specs=placed, out_specs=P("dp", "seq", None), check_vma=False
    )
```

profile of v0, /device:TPU:16, one launch (start us, length us, event | category | flops | bytes accessed | tf_op | source)
XLA Modules:
  0.0 141.2 jit_solution(805291976074449733)
XLA Ops:
  8.2 73.6 %while.45 = (s32[]{:T(128)}, bf16[64,8,128]{2,1,0:T(8,128)(2,1)S(1)}, bf16[64,8,128]{2,1,0:T(8,128)(2,1)S(1)}, bf16[9,64,8,128]{3,2,1,0:T(8,128)(2,1)S(1)}, bf16...) while((s32[]{:T(128)}, bf16[64,8,128]{2,1,0:T(8,128)(2,1)S(1)}, ...), condition=%wide.region_5.6_spmd, body=%wide.region_4.5_spmd.sunk | while | flops 6 | bytes 2097387 | solution.py:47
  10.1 3.5 %collective-permute-start = (bf16[64,8,128]{2,1,0:T(8,128)(2,1)S(1)}, bf16[64,8,128]{2,1,0:T(8,128)(2,1)S(1)}, u32[]{:S(2)}, u32[]{:S(2)}) collective-permute-start(bf16[64,8,128]{2,1,0:T(8,128)(2,1)S(1)} %get-tuple-element.517), channel_id=1, source_target_pairs={{0,1},{1,2},{2,3},{3,4},{4,5},{5,6},{6,7},{7,8},{8,9},{9,10},{10,1... | collective-permute-start | bytes 393224 | tf_op jit(solution)/shard_map/while/body/eval_jaxpr/ppermute | solution.py:17
  19.3 2.6 %collective-permute-start = (bf16[64,8,128]{2,1,0:T(8,128)(2,1)S(1)}, bf16[64,8,128]{2,1,0:T(8,128)(2,1)S(1)}, u32[]{:S(2)}, u32[]{:S(2)}) collective-permute-start(bf16[64,8,128]{2,1,0:T(8,128)(2,1)S(1)} %get-tuple-element.517), channel_id=1, source_target_pairs={{0,1},{1,2},{2,3},{3,4},{4,5},{5,6},{6,7},{7,8},{8,9},{9,10},{10,1... | collective-permute-start | bytes 393224 | tf_op jit(solution)/shard_map/while/body/eval_jaxpr/ppermute | solution.py:17
  22.0 2.6 %collective-permute-done.1 = bf16[64,8,128]{2,1,0:T(8,128)(2,1)S(1)} collective-permute-done((bf16[64,8,128]{2,1,0:T(8,128)(2,1)S(1)}, bf16[64,8,128]{2,1,0:T(8,128)(2,1)S(1)}, u32[]{:S(2)}, u32[]{:S(2)}) %collective-permute-start.1) | collective-permute-done | bytes 131104 | tf_op jit(solution)/shard_map/while/body/eval_jaxpr/ppermute | solution.py:17
  30.5 3.3 %collective-permute-done.1 = bf16[64,8,128]{2,1,0:T(8,128)(2,1)S(1)} collective-permute-done((bf16[64,8,128]{2,1,0:T(8,128)(2,1)S(1)}, bf16[64,8,128]{2,1,0:T(8,128)(2,1)S(1)}, u32[]{:S(2)}, u32[]{:S(2)}) %collective-permute-start.1) | collective-permute-done | bytes 131104 | tf_op jit(solution)/shard_map/while/body/eval_jaxpr/ppermute | solution.py:17
  39.7 3.3 %collective-permute-done.1 = bf16[64,8,128]{2,1,0:T(8,128)(2,1)S(1)} collective-permute-done((bf16[64,8,128]{2,1,0:T(8,128)(2,1)S(1)}, bf16[64,8,128]{2,1,0:T(8,128)(2,1)S(1)}, u32[]{:S(2)}, u32[]{:S(2)}) %collective-permute-start.1) | collective-permute-done | bytes 131104 | tf_op jit(solution)/shard_map/while/body/eval_jaxpr/ppermute | solution.py:17
  48.9 3.3 %collective-permute-done.1 = bf16[64,8,128]{2,1,0:T(8,128)(2,1)S(1)} collective-permute-done((bf16[64,8,128]{2,1,0:T(8,128)(2,1)S(1)}, bf16[64,8,128]{2,1,0:T(8,128)(2,1)S(1)}, u32[]{:S(2)}, u32[]{:S(2)}) %collective-permute-start.1) | collective-permute-done | bytes 131104 | tf_op jit(solution)/shard_map/while/body/eval_jaxpr/ppermute | solution.py:17
  58.1 3.3 %collective-permute-done.1 = bf16[64,8,128]{2,1,0:T(8,128)(2,1)S(1)} collective-permute-done((bf16[64,8,128]{2,1,0:T(8,128)(2,1)S(1)}, bf16[64,8,128]{2,1,0:T(8,128)(2,1)S(1)}, u32[]{:S(2)}, u32[]{:S(2)}) %collective-permute-start.1) | collective-permute-done | bytes 131104 | tf_op jit(solution)/shard_map/while/body/eval_jaxpr/ppermute | solution.py:17
  67.3 3.3 %collective-permute-done.1 = bf16[64,8,128]{2,1,0:T(8,128)(2,1)S(1)} collective-permute-done((bf16[64,8,128]{2,1,0:T(8,128)(2,1)S(1)}, bf16[64,8,128]{2,1,0:T(8,128)(2,1)S(1)}, u32[]{:S(2)}, u32[]{:S(2)}) %collective-permute-start.1) | collective-permute-done | bytes 131104 | tf_op jit(solution)/shard_map/while/body/eval_jaxpr/ppermute | solution.py:17
  76.5 3.3 %collective-permute-done.1 = bf16[64,8,128]{2,1,0:T(8,128)(2,1)S(1)} collective-permute-done((bf16[64,8,128]{2,1,0:T(8,128)(2,1)S(1)}, bf16[64,8,128]{2,1,0:T(8,128)(2,1)S(1)}, u32[]{:S(2)}, u32[]{:S(2)}) %collective-permute-start.1) | collective-permute-done | bytes 131104 | tf_op jit(solution)/shard_map/while/body/eval_jaxpr/ppermute | solution.py:17
  82.2 22.7 %while.46 = (s32[]{:T(128)}, f32[8,8,64]{2,1,0:T(8,128)S(1)}, s32[]{:T(128)}, s32[64]{0:T(128)S(1)}, bf16[9,64,8,128]{3,1,2,0:T(8,128)(2,1)S(1)}, /*index=5*/bf1...) while((s32[]{:T(128)}, f32[8,8,64]{2,1,0:T(8,128)S(1)}, ...), condition=%wide.region_8.9_spmd.clone, body=%wide.region_6.8_spmd.clone.sunk | while | flops 67907720 | bytes 1258939 | solution.py:76
  82.3 2.4 %fusion.24 = f32[8,8,64]{2,1,0:T(8,128)S(1)} fusion(bf16[64,8,8,128]{3,0,2,1:T(8,128)(2,1)} %get-tuple-element.561, pred[64,64]{0,1:T(8,128)(4,1)S(1)} %compare_and_fusion.4, bf16[9,64,8,128]{3,1,2,0:T(8,128)(2,1)S(1)} %get-tuple-element.560, s32[]{:T(128)S(6)} %select_n.57), kind=kOutput, calls=%fused_computation.5.clone.1 | convolution fusion | flops 67891200 | bytes 1204228 | tf_op jit(solution)/shard_map/while/body/qkgd,tkd->kgqt/dot_general | solution.py:67
  84.8 2.4 %fusion.24 = f32[8,8,64]{2,1,0:T(8,128)S(1)} fusion(bf16[64,8,8,128]{3,0,2,1:T(8,128)(2,1)} %get-tuple-element.561, pred[64,64]{0,1:T(8,128)(4,1)S(1)} %compare_and_fusion.4, bf16[9,64,8,128]{3,1,2,0:T(8,128)(2,1)S(1)} %get-tuple-element.560, s32[]{:T(128)S(6)} %select_n.57), kind=kOutput, calls=%fused_computation.5.clone.1 | convolution fusion | flops 67891200 | bytes 1204228 | tf_op jit(solution)/shard_map/while/body/qkgd,tkd->kgqt/dot_general | solution.py:67
  87.3 2.4 %fusion.24 = f32[8,8,64]{2,1,0:T(8,128)S(1)} fusion(bf16[64,8,8,128]{3,0,2,1:T(8,128)(2,1)} %get-tuple-element.561, pred[64,64]{0,1:T(8,128)(4,1)S(1)} %compare_and_fusion.4, bf16[9,64,8,128]{3,1,2,0:T(8,128)(2,1)S(1)} %get-tuple-element.560, s32[]{:T(128)S(6)} %select_n.57), kind=kOutput, calls=%fused_computation.5.clone.1 | convolution fusion | flops 67891200 | bytes 1204228 | tf_op jit(solution)/shard_map/while/body/qkgd,tkd->kgqt/dot_general | solution.py:67
  106.1 32.4 %while.47 = (s32[]{:T(128)}, f32[8,8,64]{2,1,0:T(8,128)S(1)}, f32[64,8,8,128]{3,0,2,1:T(8,128)S(1)}, s32[]{:T(128)}, s32[64]{0:T(128)S(1)}, /*index=5*/bf16[9,64...) while((s32[]{:T(128)}, f32[8,8,64]{2,1,0:T(8,128)S(1)}, ...), condition=%wide.region_11.12_spmd.clone, body=%wide.region_9.11_spmd.clone.sunk | while | flops 136327296 | bytes 6907351 | solution.py:93
  106.3 2.5 %convert_reduce_fusion.2 = (f32[8,8,64]{2,1,0:T(8,128)S(1)}, bf16[8,8,64,64]{2,3,1,0:T(8,128)(2,1)S(1)}) fusion(f32[8,8,64]{2,1,0:T(8,128)S(1)} %get-tuple-element.602, bf16[64,8,8,128]{3,0,2,1:T(8,128)(2,1)} %get-tuple-element.601, bf16[9,64,8,128]{3,1,2,0:T(8,128)(2,1)} %get-tuple-element.600, s32[]{:T(128)S(6)} %select_n.58, ...), kind=kOutput, calls=%fused_computation.17.clone.1 | convolution fusion | flops 68677632 | bytes 1740804 | tf_op jit(solution)/shard_map/while/body/qkgd,tkd->kgqt/dot_general | solution.py:67
  109.9 2.5 %convert_reduce_fusion.2 = (f32[8,8,64]{2,1,0:T(8,128)S(1)}, bf16[8,8,64,64]{2,3,1,0:T(8,128)(2,1)S(1)}) fusion(f32[8,8,64]{2,1,0:T(8,128)S(1)} %get-tuple-element.602, bf16[64,8,8,128]{3,0,2,1:T(8,128)(2,1)} %get-tuple-element.601, bf16[9,64,8,128]{3,1,2,0:T(8,128)(2,1)} %get-tuple-element.600, s32[]{:T(128)S(6)} %select_n.58, ...), kind=kOutput, calls=%fused_computation.17.clone.1 | convolution fusion | flops 68677632 | bytes 1740804 | tf_op jit(solution)/shard_map/while/body/qkgd,tkd->kgqt/dot_general | solution.py:67
  113.5 2.5 %convert_reduce_fusion.2 = (f32[8,8,64]{2,1,0:T(8,128)S(1)}, bf16[8,8,64,64]{2,3,1,0:T(8,128)(2,1)S(1)}) fusion(f32[8,8,64]{2,1,0:T(8,128)S(1)} %get-tuple-element.602, bf16[64,8,8,128]{3,0,2,1:T(8,128)(2,1)} %get-tuple-element.601, bf16[9,64,8,128]{3,1,2,0:T(8,128)(2,1)} %get-tuple-element.600, s32[]{:T(128)S(6)} %select_n.58, ...), kind=kOutput, calls=%fused_computation.17.clone.1 | convolution fusion | flops 68677632 | bytes 1740804 | tf_op jit(solution)/shard_map/while/body/qkgd,tkd->kgqt/dot_general | solution.py:67
  117.1 2.5 %convert_reduce_fusion.2 = (f32[8,8,64]{2,1,0:T(8,128)S(1)}, bf16[8,8,64,64]{2,3,1,0:T(8,128)(2,1)S(1)}) fusion(f32[8,8,64]{2,1,0:T(8,128)S(1)} %get-tuple-element.602, bf16[64,8,8,128]{3,0,2,1:T(8,128)(2,1)} %get-tuple-element.601, bf16[9,64,8,128]{3,1,2,0:T(8,128)(2,1)} %get-tuple-element.600, s32[]{:T(128)S(6)} %select_n.58, ...), kind=kOutput, calls=%fused_computation.17.clone.1 | convolution fusion | flops 68677632 | bytes 1740804 | tf_op jit(solution)/shard_map/while/body/qkgd,tkd->kgqt/dot_general | solution.py:67
  120.7 2.5 %convert_reduce_fusion.2 = (f32[8,8,64]{2,1,0:T(8,128)S(1)}, bf16[8,8,64,64]{2,3,1,0:T(8,128)(2,1)S(1)}) fusion(f32[8,8,64]{2,1,0:T(8,128)S(1)} %get-tuple-element.602, bf16[64,8,8,128]{3,0,2,1:T(8,128)(2,1)} %get-tuple-element.601, bf16[9,64,8,128]{3,1,2,0:T(8,128)(2,1)} %get-tuple-element.600, s32[]{:T(128)S(6)} %select_n.58, ...), kind=kOutput, calls=%fused_computation.17.clone.1 | convolution fusion | flops 68677632 | bytes 1740804 | tf_op jit(solution)/shard_map/while/body/qkgd,tkd->kgqt/dot_general | solution.py:67
  124.3 2.5 %convert_reduce_fusion.2 = (f32[8,8,64]{2,1,0:T(8,128)S(1)}, bf16[8,8,64,64]{2,3,1,0:T(8,128)(2,1)S(1)}) fusion(f32[8,8,64]{2,1,0:T(8,128)S(1)} %get-tuple-element.602, bf16[64,8,8,128]{3,0,2,1:T(8,128)(2,1)} %get-tuple-element.601, bf16[9,64,8,128]{3,1,2,0:T(8,128)(2,1)} %get-tuple-element.600, s32[]{:T(128)S(6)} %select_n.58, ...), kind=kOutput, calls=%fused_computation.17.clone.1 | convolution fusion | flops 68677632 | bytes 1740804 | tf_op jit(solution)/shard_map/while/body/qkgd,tkd->kgqt/dot_general | solution.py:67
  127.9 2.5 %convert_reduce_fusion.2 = (f32[8,8,64]{2,1,0:T(8,128)S(1)}, bf16[8,8,64,64]{2,3,1,0:T(8,128)(2,1)S(1)}) fusion(f32[8,8,64]{2,1,0:T(8,128)S(1)} %get-tuple-element.602, bf16[64,8,8,128]{3,0,2,1:T(8,128)(2,1)} %get-tuple-element.601, bf16[9,64,8,128]{3,1,2,0:T(8,128)(2,1)} %get-tuple-element.600, s32[]{:T(128)S(6)} %select_n.58, ...), kind=kOutput, calls=%fused_computation.17.clone.1 | convolution fusion | flops 68677632 | bytes 1740804 | tf_op jit(solution)/shard_map/while/body/qkgd,tkd->kgqt/dot_general | solution.py:67
  131.4 2.5 %convert_reduce_fusion.2 = (f32[8,8,64]{2,1,0:T(8,128)S(1)}, bf16[8,8,64,64]{2,3,1,0:T(8,128)(2,1)S(1)}) fusion(f32[8,8,64]{2,1,0:T(8,128)S(1)} %get-tuple-element.602, bf16[64,8,8,128]{3,0,2,1:T(8,128)(2,1)} %get-tuple-element.601, bf16[9,64,8,128]{3,1,2,0:T(8,128)(2,1)} %get-tuple-element.600, s32[]{:T(128)S(6)} %select_n.58, ...), kind=kOutput, calls=%fused_computation.17.clone.1 | convolution fusion | flops 68677632 | bytes 1740804 | tf_op jit(solution)/shard_map/while/body/qkgd,tkd->kgqt/dot_general | solution.py:67
  135.0 2.5 %convert_reduce_fusion.2 = (f32[8,8,64]{2,1,0:T(8,128)S(1)}, bf16[8,8,64,64]{2,3,1,0:T(8,128)(2,1)S(1)}) fusion(f32[8,8,64]{2,1,0:T(8,128)S(1)} %get-tuple-element.602, bf16[64,8,8,128]{3,0,2,1:T(8,128)(2,1)} %get-tuple-element.601, bf16[9,64,8,128]{3,1,2,0:T(8,128)(2,1)} %get-tuple-element.600, s32[]{:T(128)S(6)} %select_n.58, ...), kind=kOutput, calls=%fused_computation.17.clone.1 | convolution fusion | flops 68677632 | bytes 1740804 | tf_op jit(solution)/shard_map/while/body/qkgd,tkd->kgqt/dot_general | solution.py:67
  (160 shorter events, 80.8 us)
Async XLA Ops:
  0.0 0.7 copy-start
  8.2 7.2 %collective-permute-start.1 = (bf16[64,8,128]{2,1,0:T(8,128)(2,1)S(1)}, bf16[64,8,128]{2,1,0:T(8,128)(2,1)S(1)}, u32[]{:S(2)}, u32[]{:S(2)}) collective-permute-start(bf16[64,8,128]{2,1,0:T(8,128)(2,1)S(1)} %get-tuple-element.518), channel_id=1, source_target_pairs={{0,1},{1,2},{2,3},{3,4},{4,5},{5,6},{6,7},{7,8},{8,9},{9,10},{10,1... | collective-permute-start | bytes 393224 | tf_op jit(solution)/shard_map/while/body/eval_jaxpr/ppermute | solution.py:17
  10.1 7.2 %collective-permute-start = (bf16[64,8,128]{2,1,0:T(8,128)(2,1)S(1)}, bf16[64,8,128]{2,1,0:T(8,128)(2,1)S(1)}, u32[]{:S(2)}, u32[]{:S(2)}) collective-permute-start(bf16[64,8,128]{2,1,0:T(8,128)(2,1)S(1)} %get-tuple-element.517), channel_id=1, source_target_pairs={{0,1},{1,2},{2,3},{3,4},{4,5},{5,6},{6,7},{7,8},{8,9},{9,10},{10,1... | collective-permute-start | bytes 393224 | tf_op jit(solution)/shard_map/while/body/eval_jaxpr/ppermute | solution.py:17
  17.4 7.2 %collective-permute-start.1 = (bf16[64,8,128]{2,1,0:T(8,128)(2,1)S(1)}, bf16[64,8,128]{2,1,0:T(8,128)(2,1)S(1)}, u32[]{:S(2)}, u32[]{:S(2)}) collective-permute-start(bf16[64,8,128]{2,1,0:T(8,128)(2,1)S(1)} %get-tuple-element.518), channel_id=1, source_target_pairs={{0,1},{1,2},{2,3},{3,4},{4,5},{5,6},{6,7},{7,8},{8,9},{9,10},{10,1... | collective-permute-start | bytes 393224 | tf_op jit(solution)/shard_map/while/body/eval_jaxpr/ppermute | solution.py:17
  19.3 7.2 %collective-permute-start = (bf16[64,8,128]{2,1,0:T(8,128)(2,1)S(1)}, bf16[64,8,128]{2,1,0:T(8,128)(2,1)S(1)}, u32[]{:S(2)}, u32[]{:S(2)}) collective-permute-start(bf16[64,8,128]{2,1,0:T(8,128)(2,1)S(1)} %get-tuple-element.517), channel_id=1, source_target_pairs={{0,1},{1,2},{2,3},{3,4},{4,5},{5,6},{6,7},{7,8},{8,9},{9,10},{10,1... | collective-permute-start | bytes 393224 | tf_op jit(solution)/shard_map/while/body/eval_jaxpr/ppermute | solution.py:17
  26.6 7.2 %collective-permute-start.1 = (bf16[64,8,128]{2,1,0:T(8,128)(2,1)S(1)}, bf16[64,8,128]{2,1,0:T(8,128)(2,1)S(1)}, u32[]{:S(2)}, u32[]{:S(2)}) collective-permute-start(bf16[64,8,128]{2,1,0:T(8,128)(2,1)S(1)} %get-tuple-element.518), channel_id=1, source_target_pairs={{0,1},{1,2},{2,3},{3,4},{4,5},{5,6},{6,7},{7,8},{8,9},{9,10},{10,1... | collective-permute-start | bytes 393224 | tf_op jit(solution)/shard_map/while/body/eval_jaxpr/ppermute | solution.py:17
  28.5 7.2 %collective-permute-start = (bf16[64,8,128]{2,1,0:T(8,128)(2,1)S(1)}, bf16[64,8,128]{2,1,0:T(8,128)(2,1)S(1)}, u32[]{:S(2)}, u32[]{:S(2)}) collective-permute-start(bf16[64,8,128]{2,1,0:T(8,128)(2,1)S(1)} %get-tuple-element.517), channel_id=1, source_target_pairs={{0,1},{1,2},{2,3},{3,4},{4,5},{5,6},{6,7},{7,8},{8,9},{9,10},{10,1... | collective-permute-start | bytes 393224 | tf_op jit(solution)/shard_map/while/body/eval_jaxpr/ppermute | solution.py:17
  35.8 7.2 %collective-permute-start.1 = (bf16[64,8,128]{2,1,0:T(8,128)(2,1)S(1)}, bf16[64,8,128]{2,1,0:T(8,128)(2,1)S(1)}, u32[]{:S(2)}, u32[]{:S(2)}) collective-permute-start(bf16[64,8,128]{2,1,0:T(8,128)(2,1)S(1)} %get-tuple-element.518), channel_id=1, source_target_pairs={{0,1},{1,2},{2,3},{3,4},{4,5},{5,6},{6,7},{7,8},{8,9},{9,10},{10,1... | collective-permute-start | bytes 393224 | tf_op jit(solution)/shard_map/while/body/eval_jaxpr/ppermute | solution.py:17
  37.7 7.2 %collective-permute-start = (bf16[64,8,128]{2,1,0:T(8,128)(2,1)S(1)}, bf16[64,8,128]{2,1,0:T(8,128)(2,1)S(1)}, u32[]{:S(2)}, u32[]{:S(2)}) collective-permute-start(bf16[64,8,128]{2,1,0:T(8,128)(2,1)S(1)} %get-tuple-element.517), channel_id=1, source_target_pairs={{0,1},{1,2},{2,3},{3,4},{4,5},{5,6},{6,7},{7,8},{8,9},{9,10},{10,1... | collective-permute-start | bytes 393224 | tf_op jit(solution)/shard_map/while/body/eval_jaxpr/ppermute | solution.py:17
  45.0 7.2 %collective-permute-start.1 = (bf16[64,8,128]{2,1,0:T(8,128)(2,1)S(1)}, bf16[64,8,128]{2,1,0:T(8,128)(2,1)S(1)}, u32[]{:S(2)}, u32[]{:S(2)}) collective-permute-start(bf16[64,8,128]{2,1,0:T(8,128)(2,1)S(1)} %get-tuple-element.518), channel_id=1, source_target_pairs={{0,1},{1,2},{2,3},{3,4},{4,5},{5,6},{6,7},{7,8},{8,9},{9,10},{10,1... | collective-permute-start | bytes 393224 | tf_op jit(solution)/shard_map/while/body/eval_jaxpr/ppermute | solution.py:17
  46.9 7.2 %collective-permute-start = (bf16[64,8,128]{2,1,0:T(8,128)(2,1)S(1)}, bf16[64,8,128]{2,1,0:T(8,128)(2,1)S(1)}, u32[]{:S(2)}, u32[]{:S(2)}) collective-permute-start(bf16[64,8,128]{2,1,0:T(8,128)(2,1)S(1)} %get-tuple-element.517), channel_id=1, source_target_pairs={{0,1},{1,2},{2,3},{3,4},{4,5},{5,6},{6,7},{7,8},{8,9},{9,10},{10,1... | collective-permute-start | bytes 393224 | tf_op jit(solution)/shard_map/while/body/eval_jaxpr/ppermute | solution.py:17
  54.2 7.2 %collective-permute-start.1 = (bf16[64,8,128]{2,1,0:T(8,128)(2,1)S(1)}, bf16[64,8,128]{2,1,0:T(8,128)(2,1)S(1)}, u32[]{:S(2)}, u32[]{:S(2)}) collective-permute-start(bf16[64,8,128]{2,1,0:T(8,128)(2,1)S(1)} %get-tuple-element.518), channel_id=1, source_target_pairs={{0,1},{1,2},{2,3},{3,4},{4,5},{5,6},{6,7},{7,8},{8,9},{9,10},{10,1... | collective-permute-start | bytes 393224 | tf_op jit(solution)/shard_map/while/body/eval_jaxpr/ppermute | solution.py:17
  56.2 7.2 %collective-permute-start = (bf16[64,8,128]{2,1,0:T(8,128)(2,1)S(1)}, bf16[64,8,128]{2,1,0:T(8,128)(2,1)S(1)}, u32[]{:S(2)}, u32[]{:S(2)}) collective-permute-start(bf16[64,8,128]{2,1,0:T(8,128)(2,1)S(1)} %get-tuple-element.517), channel_id=1, source_target_pairs={{0,1},{1,2},{2,3},{3,4},{4,5},{5,6},{6,7},{7,8},{8,9},{9,10},{10,1... | collective-permute-start | bytes 393224 | tf_op jit(solution)/shard_map/while/body/eval_jaxpr/ppermute | solution.py:17
  63.4 7.2 %collective-permute-start.1 = (bf16[64,8,128]{2,1,0:T(8,128)(2,1)S(1)}, bf16[64,8,128]{2,1,0:T(8,128)(2,1)S(1)}, u32[]{:S(2)}, u32[]{:S(2)}) collective-permute-start(bf16[64,8,128]{2,1,0:T(8,128)(2,1)S(1)} %get-tuple-element.518), channel_id=1, source_target_pairs={{0,1},{1,2},{2,3},{3,4},{4,5},{5,6},{6,7},{7,8},{8,9},{9,10},{10,1... | collective-permute-start | bytes 393224 | tf_op jit(solution)/shard_map/while/body/eval_jaxpr/ppermute | solution.py:17
  65.4 7.2 %collective-permute-start = (bf16[64,8,128]{2,1,0:T(8,128)(2,1)S(1)}, bf16[64,8,128]{2,1,0:T(8,128)(2,1)S(1)}, u32[]{:S(2)}, u32[]{:S(2)}) collective-permute-start(bf16[64,8,128]{2,1,0:T(8,128)(2,1)S(1)} %get-tuple-element.517), channel_id=1, source_target_pairs={{0,1},{1,2},{2,3},{3,4},{4,5},{5,6},{6,7},{7,8},{8,9},{9,10},{10,1... | collective-permute-start | bytes 393224 | tf_op jit(solution)/shard_map/while/body/eval_jaxpr/ppermute | solution.py:17
  72.6 7.2 %collective-permute-start.1 = (bf16[64,8,128]{2,1,0:T(8,128)(2,1)S(1)}, bf16[64,8,128]{2,1,0:T(8,128)(2,1)S(1)}, u32[]{:S(2)}, u32[]{:S(2)}) collective-permute-start(bf16[64,8,128]{2,1,0:T(8,128)(2,1)S(1)} %get-tuple-element.518), channel_id=1, source_target_pairs={{0,1},{1,2},{2,3},{3,4},{4,5},{5,6},{6,7},{7,8},{8,9},{9,10},{10,1... | collective-permute-start | bytes 393224 | tf_op jit(solution)/shard_map/while/body/eval_jaxpr/ppermute | solution.py:17
  74.6 7.2 %collective-permute-start = (bf16[64,8,128]{2,1,0:T(8,128)(2,1)S(1)}, bf16[64,8,128]{2,1,0:T(8,128)(2,1)S(1)}, u32[]{:S(2)}, u32[]{:S(2)}) collective-permute-start(bf16[64,8,128]{2,1,0:T(8,128)(2,1)S(1)} %get-tuple-element.517), channel_id=1, source_target_pairs={{0,1},{1,2},{2,3},{3,4},{4,5},{5,6},{6,7},{7,8},{8,9},{9,10},{10,1... | collective-permute-start | bytes 393224 | tf_op jit(solution)/shard_map/while/body/eval_jaxpr/ppermute | solution.py:17
  104.9 1.0 copy-start.1
where the time goes:
time: 142 us; the launch traced here: 141 us
  matrix products  52.2 us (37%)
  waiting for transfers between devices  39.6 us (28%)
  starting transfers between devices  33 us (23%)
  local copies, waits for them, and re-layouts  10.4 us (7%)
  other arithmetic  3.55 us (2%)
  loops' own time  1.62 us (1%)
    dot_general x18, matrix products, tile(): jnp.einsum('qkgd,tkd->kgqt', grouped, key_tile, preferred_element_type=jn...  43.6 us
    ppermute x16, waiting for transfers between devices, shifted(): return lax.ppermute(block, axis, route)  39.6 us
    ppermute x16, starting transfers between devices, shifted(): return lax.ppermute(block, axis, route)  33 us
    dot_general x9, matrix products, sum_step(): jnp.einsum('kgqt,tkd->qkgd', weights, value_tile, preferred_element_type=...  8.61 us
    unnamed x9, local copies, waits for them, and re-layouts  6.99 us
  transfers between devices with their start and end apart: 16, of which 16 were waited for; matrix products, arithmetic and copies ran while one was open for 0% of the time, Pallas kernels for 0%

commit v1 on v0

v1 whole, which is shorter than its diff:
```python
import functools
import math

import jax
import jax.numpy as jnp
from jax import lax
from jax.experimental import pallas as pl
from jax.experimental.pallas import tpu as pltpu
from jax.sharding import PartitionSpec as P

QH = 64
KVH = 8
HD = 128
GROUP = 8
MASKED = -1e30


def doc_starts(lengths_row, positions):
    doc_ends = jnp.cumsum(lengths_row)
    return jnp.max(jnp.where(doc_ends[None, :] <= positions[:, None], doc_ends, 0), axis=1)


def attend(first_row, rows, blocks, bases, first_position, starts, q, kv, bias, out):
    tokens = kv.shape[1]
    exponent_scale = math.log2(math.e) / math.sqrt(HD)
    span = slice(first_row, first_row + rows)
    width = tokens * len(blocks)
    row_position = (
        first_position + first_row + lax.broadcasted_iota(jnp.int32, (rows, tokens), 0)
    )
    column = lax.broadcasted_iota(jnp.int32, (rows, tokens), 1)
    begin = starts[span, :tokens]
    for slot, base in enumerate(bases):
        key_position = base + column
        allowed = (key_position >= begin) & (key_position <= row_position)
        bias[span, slot * tokens : (slot + 1) * tokens] = jnp.where(allowed, 0.0, MASKED)
    mask = bias[span, :width]
    wide_mask = jnp.concatenate([mask] * GROUP, axis=0)
    ones = jnp.ones((width, HD), jnp.bfloat16)
    for g in range(KVH):
        columns = slice(g * HD, (g + 1) * HD)
        value_columns = slice((KVH + g) * HD, (KVH + g + 1) * HD)
        q_rows = jnp.concatenate(
            [q[span, (g * GROUP + h) * HD : (g * GROUP + h + 1) * HD] for h in range(GROUP)],
            axis=0,
        )
        k = jnp.concatenate([kv[b, :, columns] for b in blocks], axis=0)
        v = jnp.concatenate([kv[b, :, value_columns] for b in blocks], axis=0)
        v = jnp.concatenate([v, ones], axis=1)
        scores = (
            lax.dot_general(q_rows, k, (((1,), (1,)), ((), ())), preferred_element_type=jnp.float32)
            + wide_mask
        )
        peak = jnp.max(scores, axis=1, keepdims=True)
        weights = jnp.exp2((scores - peak) * exponent_scale).astype(jnp.bfloat16)
        summed = jnp.dot(weights, v, preferred_element_type=jnp.float32)
        result = (summed[:, :HD] / summed[:, HD:]).astype(jnp.bfloat16)
        for h in range(GROUP):
            out[span, (g * GROUP + h) * HD : (g * GROUP + h + 1) * HD] = result[
                h * rows : (h + 1) * rows
            ]


def attention_kernel(group, near, far, *refs):
    pairs = 1 + len(near) + len(far)
    starts, q_hbm = refs[:2]
    kv_hbm = refs[2 : 2 + 2 * pairs]
    out_hbm = refs[2 + 2 * pairs]
    q, kv, bias, out, sems = refs[3 + 2 * pairs :]
    tokens = q.shape[0]
    copies = [pltpu.make_async_copy(q_hbm, q, sems.at[2 * pairs])]
    copies += [
        pltpu.make_async_copy(kv_hbm[b], kv.at[b], sems.at[b]) for b in range(2 * pairs)
    ]
    for copy in copies:
        copy.start()
    for copy in copies:
        copy.wait()
    index = lax.axis_index("seq")
    pair, core = index // 2, index % 2
    first_position = index * tokens
    never = jnp.int32(1 << 30)

    def base_of(distance, valid):
        source = (pair - distance) * 2
        return [
            jnp.where(valid, (source + core) * tokens, never),
            jnp.where(valid, (source + 1 - core) * tokens, never),
        ]

    lowest = jnp.where(pair <= group, 0, group)
    within = functools.partial(
        attend, first_position=first_position, starts=starts, q=q, kv=kv, bias=bias, out=out
    )

    @pl.when(pair != group)
    def _():
        bases = base_of(0, True)
        for d in near:
            bases += base_of(d, pair - d >= lowest)
        within(0, tokens, range(2 * (1 + len(near))), bases)

    @pl.when(pair == group)
    def _():
        blocks, bases = [0, 1], base_of(0, True)
        for slot, d in enumerate(near):
            if d <= group // 2:
                blocks += [2 + 2 * slot, 3 + 2 * slot]
                bases += base_of(d, True)
        for slot, d in enumerate(far):
            blocks += [2 + 2 * len(near) + 2 * slot, 3 + 2 * len(near) + 2 * slot]
            bases += base_of(d, True)
        within(0, tokens // 2, blocks, bases)
        within(tokens // 2, tokens // 2, [0, 1], base_of(0, True))

    copy = pltpu.make_async_copy(out, out_hbm, sems.at[2 * pairs])
    copy.start()
    copy.wait()


def per_device(queries, keys, values, doc_lengths):
    tokens = queries.shape[1]
    seq_count = lax.axis_size("seq")
    pairs = seq_count // 2
    group = pairs // 2
    half = group // 2
    index = lax.axis_index("seq")

    def send(block, routes):
        devices = [(2 * a + core, 2 * b + core) for a, b in routes for core in (0, 1)]
        return lax.ppermute(block, "seq", devices)

    def swap(block):
        return lax.ppermute(block, "seq", [(i, i ^ 1) for i in range(seq_count)])

    own = jnp.concatenate([keys[0], values[0]], axis=1)
    near = [half] + [d for d in range(1, group) if d != half]
    far = list(range(half + 1, group + 1))
    received = {}
    for d in near:
        routes = [(p - d, p) for p in range(d, group)]
        routes += [(p - d, p) for p in range(group + d, pairs)]
        if d <= half:
            routes.append((group - d, group))
        received[d] = send(own, routes)
    passed = [send(received[half], [(group - d + half, group)]) for d in far]
    blocks = []
    for block in [own] + [received[d] for d in near] + passed:
        blocks += [block, swap(block)]
    lengths_row = lax.dynamic_index_in_dim(doc_lengths, lax.axis_index("dp"), 0, keepdims=False)
    positions = index * tokens + jnp.arange(tokens, dtype=jnp.int32)
    starts = jnp.broadcast_to(doc_starts(lengths_row, positions)[:, None], (tokens, 128))
    any_spec = pl.BlockSpec(memory_space=pl.ANY)
    out = pl.pallas_call(
        functools.partial(attention_kernel, group, near, far),
        out_shape=jax.ShapeDtypeStruct((tokens, QH * HD), jnp.bfloat16),
        in_specs=[pl.BlockSpec(memory_space=pltpu.VMEM)] + [any_spec] * (1 + len(blocks)),
        out_specs=any_spec,
        scratch_shapes=[
            pltpu.VMEM((tokens, QH * HD), jnp.bfloat16),
            pltpu.VMEM((len(blocks), tokens, 2 * KVH * HD), jnp.bfloat16),
            pltpu.VMEM((tokens, tokens * len(blocks)), jnp.float32),
            pltpu.VMEM((tokens, QH * HD), jnp.bfloat16),
            pltpu.SemaphoreType.DMA((len(blocks) + 1,)),
        ],
        compiler_params=pltpu.CompilerParams(vmem_limit_bytes=48 * 1024 * 1024),
    )(starts, queries[0], *blocks)
    return out[None]


def solution(mesh):
    placed = (P("dp", "seq", None), P("dp", "seq", None), P("dp", "seq", None), P())
    return jax.shard_map(
        per_device, mesh=mesh, in_specs=placed, out_specs=P("dp", "seq", None), check_vma=False
    )
```

time: 142 us -> 31.5 us (0.22)
  matrix products: 52.2 us -> 0 us
  waiting for transfers between devices: 39.6 us -> 11.7 us
  starting transfers between devices: 33 us -> 10.8 us
  local copies, waits for them, and re-layouts: 10.4 us -> 1.51 us
  Pallas kernels: 0 us -> 5.16 us
  other arithmetic: 3.55 us -> 1.6 us
  loops' own time: 1.62 us -> 0 us
    dot_general x27 -> x0, matrix products: 52.2 us -> none  [the longest x18 43.6 us: tile(): jnp.einsum('qkgd,tkd->kgqt', grouped, key_tile, preferred_element_type=jn...]
    ppermute x16 -> x11, waiting for transfers between devices: 39.6 us -> 11.7 us  [the longest x5 10.5 us: send(): return lax.ppermute(block, 'seq', devices)]
    ppermute x16 -> x11, starting transfers between devices: 33 us -> 10.8 us  [the longest x5 10.2 us: send(): return lax.ppermute(block, 'seq', devices)]
    unnamed x9 -> x4, local copies, waits for them, and re-layouts: 6.99 us -> 1.23 us
    pallas_call x0 -> x1, Pallas kernels: none -> 5.16 us  [per_device(): pl.pallas_call(functools.partial(attention_kernel, group, near, far), out...]
    another operation x3 -> x0, loops' own time: 1.62 us -> none  [the longest x1 0.63 us: per_device(): lax.fori_loop(first_slot, reach + 1, sum_step, (jnp.zeros((KVH, GROUP, to...]
  transfers between devices with their start and end apart: 16 -> 11, of which waited for: 16 -> 6; matrix products, arithmetic and copies ran while one was open for 0% -> 3% of each run, Pallas kernels for 0% -> 0%
where the time goes in v1:
time: 31.5 us; the launch traced here: 30.9 us
  waiting for transfers between devices  11.7 us (37%)
  starting transfers between devices  10.8 us (34%)
  Pallas kernels  5.16 us (16%)
  other arithmetic  1.6 us (5%)
  local copies, waits for them, and re-layouts  1.51 us (5%)
    ppermute x5, waiting for transfers between devices, send(): return lax.ppermute(block, 'seq', devices)  10.5 us
    ppermute x5, starting transfers between devices, send(): return lax.ppermute(block, 'seq', devices)  10.2 us
    pallas_call x1, Pallas kernels, per_device(): pl.pallas_call(functools.partial(attention_kernel, group, near, far), out...  5.16 us
    ppermute x6, waiting for transfers between devices, swap(): return lax.ppermute(block, 'seq', [(i, i ^ 1) for i in range(seq_count)])  1.24 us
    unnamed x4, local copies, waits for them, and re-layouts  1.23 us
    concatenate x1, other arithmetic, per_device(): own = jnp.concatenate([keys[0], values[0]], axis=1)  1 us
  transfers between devices with their start and end apart: 11, of which 6 were waited for; matrix products, arithmetic and copies ran while one was open for 3% of the time, Pallas kernels for 0%

profile of v1, /device:TPU:16, one launch (start us, length us, event | category | flops | bytes accessed | tf_op | source)
XLA Modules:
  0.0 30.9 jit_solution(3385009516607045929)
XLA Ops:
  0.0 1.0 %pad_maximum_fusion.refs_2_ = bf16[64,2048]{1,0:T(8,128)(2,1)S(1)} fusion(bf16[64,1024]{1,0:T(8,128)(2,1)} %bitcast.11, bf16[64,1024]{1,0:T(8,128)(2,1)} %bitcast.12), kind=kLoop, calls=%fused_computation | loop fusion | flops 524288 | bytes 524288 | tf_op jit(solution)/shard_map/concatenate | solution.py:136
  1.0 3.5 %collective-permute-start.1 = (bf16[64,2048]{1,0:T(8,128)(2,1)S(1)}, bf16[64,2048]{1,0:T(8,128)(2,1)S(1)}, u32[]{:S(2)}, u32[]{:S(2)}) collective-permute-start(bf16[64,2048]{1,0:T(8,128)(2,1)S(1)} %pad_maximum_fusion.refs_2_), channel_id=1, source_target_pairs={{0,4},{1,5},{2,6},{3,7},{8,12},{9,13},{10,14},{11,15},{4,8},{5,9},... | collective-permute-start | bytes 786440 | tf_op jit(solution)/shard_map/ppermute | solution.py:131
  4.5 2.2 %collective-permute-start.5 = (bf16[64,2048]{1,0:T(8,128)(2,1)S(1)}, bf16[64,2048]{1,0:T(8,128)(2,1)S(1)}, u32[]{:S(2)}, u32[]{:S(2)}) collective-permute-start(bf16[64,2048]{1,0:T(8,128)(2,1)S(1)} %pad_maximum_fusion.refs_2_), channel_id=1, source_target_pairs={{0,6},{1,7},{8,14},{9,15},{16,22},{17,23},{24,30},{25,31}} | collective-permute-start | bytes 786440 | tf_op jit(solution)/shard_map/ppermute | solution.py:131
  6.7 1.9 %collective-permute-start.3 = (bf16[64,2048]{1,0:T(8,128)(2,1)S(1)}, bf16[64,2048]{1,0:T(8,128)(2,1)S(1)}, u32[]{:S(2)}, u32[]{:S(2)}) collective-permute-start(bf16[64,2048]{1,0:T(8,128)(2,1)S(1)} %pad_maximum_fusion.refs_2_), channel_id=1, source_target_pairs={{0,2},{1,3},{2,4},{3,5},{4,6},{5,7},{8,10},{9,11},{10,12},{11,13},... | collective-permute-start | bytes 786440 | tf_op jit(solution)/shard_map/ppermute | solution.py:131
  8.7 0.1 collective-permute-start
  8.7 2.4 %collective-permute-done.1.refs_4_ = bf16[64,2048]{1,0:T(8,128)(2,1)S(1)} collective-permute-done((bf16[64,2048]{1,0:T(8,128)(2,1)S(1)}, bf16[64,2048]{1,0:T(8,128)(2,1)S(1)}, u32[]{:S(2)}, u32[]{:S(2)}) %collective-permute-start.1) | collective-permute-done | bytes 262176 | tf_op jit(solution)/shard_map/ppermute | solution.py:131
  11.2 1.3 %collective-permute-start.9 = (bf16[64,2048]{1,0:T(8,128)(2,1)S(1)}, bf16[64,2048]{1,0:T(8,128)(2,1)S(1)}, u32[]{:S(2)}, u32[]{:S(2)}) collective-permute-start(bf16[64,2048]{1,0:T(8,128)(2,1)S(1)} %collective-permute-done.1.refs_4_), channel_id=1, source_target_pairs={{4,8},{5,9},{20,24},{21,25}} | collective-permute-start | bytes 786440 | tf_op jit(solution)/shard_map/ppermute | solution.py:131
  12.5 1.3 %collective-permute-start.7 = (bf16[64,2048]{1,0:T(8,128)(2,1)S(1)}, bf16[64,2048]{1,0:T(8,128)(2,1)S(1)}, u32[]{:S(2)}, u32[]{:S(2)}) collective-permute-start(bf16[64,2048]{1,0:T(8,128)(2,1)S(1)} %collective-permute-done.1.refs_4_), channel_id=1, source_target_pairs={{6,8},{7,9},{22,24},{23,25}} | collective-permute-start | bytes 786440 | tf_op jit(solution)/shard_map/ppermute | solution.py:131
  13.8 0.3 reduce-window.9
  14.1 0.1 slice.10
  14.2 0.1 slice_reduce_fusion
  14.3 1.4 %collective-permute-done.5.refs_8_ = bf16[64,2048]{1,0:T(8,128)(2,1)S(1)} collective-permute-done((bf16[64,2048]{1,0:T(8,128)(2,1)S(1)}, bf16[64,2048]{1,0:T(8,128)(2,1)S(1)}, u32[]{:S(2)}, u32[]{:S(2)}) %collective-permute-start.5) | collective-permute-done | bytes 262176 | tf_op jit(solution)/shard_map/ppermute | solution.py:131
  15.7 0.0 collective-permute-start.2
  15.7 2.2 %collective-permute-done.3.refs_6_ = bf16[64,2048]{1,0:T(8,128)(2,1)S(1)} collective-permute-done((bf16[64,2048]{1,0:T(8,128)(2,1)S(1)}, bf16[64,2048]{1,0:T(8,128)(2,1)S(1)}, u32[]{:S(2)}, u32[]{:S(2)}) %collective-permute-start.3) | collective-permute-done | bytes 262176 | tf_op jit(solution)/shard_map/ppermute | solution.py:131
  17.9 0.5 %collective-permute-start.4 = (bf16[64,2048]{1,0:T(8,128)(2,1)S(1)}, bf16[64,2048]{1,0:T(8,128)(2,1)S(1)}, u32[]{:S(2)}, u32[]{:S(2)}) collective-permute-start(bf16[64,2048]{1,0:T(8,128)(2,1)S(1)} %collective-permute-done.3.refs_6_), channel_id=1, source_target_pairs={{0,1},{1,0},{2,3},{3,2},{4,5},{5,4},{6,7},{7,6},{8,9},{9,8},{10,11... | collective-permute-start | bytes 786440 | tf_op jit(solution)/shard_map/ppermute | solution.py:134
  18.5 1.5 %collective-permute-done.9.refs_12_ = bf16[64,2048]{1,0:T(8,128)(2,1)S(1)} collective-permute-done((bf16[64,2048]{1,0:T(8,128)(2,1)S(1)}, bf16[64,2048]{1,0:T(8,128)(2,1)S(1)}, u32[]{:S(2)}, u32[]{:S(2)}) %collective-permute-start.9) | collective-permute-done | bytes 262176 | tf_op jit(solution)/shard_map/ppermute | solution.py:131
  20.0 0.0 collective-permute-start.10
  20.0 2.9 %collective-permute-done.7.refs_10_ = bf16[64,2048]{1,0:T(8,128)(2,1)S(1)} collective-permute-done((bf16[64,2048]{1,0:T(8,128)(2,1)S(1)}, bf16[64,2048]{1,0:T(8,128)(2,1)S(1)}, u32[]{:S(2)}, u32[]{:S(2)}) %collective-permute-start.7) | collective-permute-done | bytes 262176 | tf_op jit(solution)/shard_map/ppermute | solution.py:131
  22.9 0.1 add_bitcast_fusion
  23.0 0.2 select_reduce_fusion
  23.2 1.2 %collective-permute-done.8.refs_11_ = bf16[64,2048]{1,0:T(8,128)(2,1)S(1)} collective-permute-done((bf16[64,2048]{1,0:T(8,128)(2,1)S(1)}, bf16[64,2048]{1,0:T(8,128)(2,1)S(1)}, u32[]{:S(2)}, u32[]{:S(2)}) %collective-permute-start.8) | collective-permute-done | bytes 262176 | tf_op jit(solution)/shard_map/ppermute | solution.py:134
  24.4 0.1 broadcast_in_dim.18.refs_0_
  24.5 1.2 %copy-done.1 = bf16[1,64,8192]{2,1,0:T(8,128)(2,1)S(1)} copy-done((bf16[1,64,8192]{2,1,0:T(8,128)(2,1)S(1)}, bf16[1,64,8192]{2,1,0:T(8,128)(2,1)}, u32[]{:S(2)}) %copy-start.1) | copy-done | bytes 1048600
  25.8 5.2 %shard_map.46 = bf16[64,8192]{1,0:T(8,128)(2,1)} custom-call(s32[64,128]{1,0:T(8,128)S(1)} %broadcast_in_dim.18.refs_0_, bf16[64,8192]{1,0:T(8,128)(2,1)S(1)} %bitcast.10, bf16[64,2048]{1,0:T(8,128)(2,1)S(1)} %pad_maximum_fusion.refs_2_, bf16[64,2048]{1,0:T(8,128)(2,1)S(1)} %collective-permute-done.refs_3_, ...), custom_call_target="tpu_custom_call" | custom-call | tf_op jit(solution)/shard_map/pallas_call | solution.py:154
  (14 shorter events, 0.1 us)
Async XLA Ops:
  0.0 13.8 %copy-start = (s32[2,129]{1,0:T(2,128)S(1)}, s32[2,129]{1,0:T(2,128)}, u32[]{:S(2)}) copy-start(s32[2,129]{1,0:T(2,128)} %param.7) | copy-start | bytes 3100
  1.0 10.2 %collective-permute-start.1 = (bf16[64,2048]{1,0:T(8,128)(2,1)S(1)}, bf16[64,2048]{1,0:T(8,128)(2,1)S(1)}, u32[]{:S(2)}, u32[]{:S(2)}) collective-permute-start(bf16[64,2048]{1,0:T(8,128)(2,1)S(1)} %pad_maximum_fusion.refs_2_), channel_id=1, source_target_pairs={{0,4},{1,5},{2,6},{3,7},{8,12},{9,13},{10,14},{11,15},{4,8},{5,9},... | collective-permute-start | bytes 786440 | tf_op jit(solution)/shard_map/ppermute | solution.py:131
  4.5 11.2 %collective-permute-start.5 = (bf16[64,2048]{1,0:T(8,128)(2,1)S(1)}, bf16[64,2048]{1,0:T(8,128)(2,1)S(1)}, u32[]{:S(2)}, u32[]{:S(2)}) collective-permute-start(bf16[64,2048]{1,0:T(8,128)(2,1)S(1)} %pad_maximum_fusion.refs_2_), channel_id=1, source_target_pairs={{0,6},{1,7},{8,14},{9,15},{16,22},{17,23},{24,30},{25,31}} | collective-permute-start | bytes 786440 | tf_op jit(solution)/shard_map/ppermute | solution.py:131
  6.7 11.2 %collective-permute-start.3 = (bf16[64,2048]{1,0:T(8,128)(2,1)S(1)}, bf16[64,2048]{1,0:T(8,128)(2,1)S(1)}, u32[]{:S(2)}, u32[]{:S(2)}) collective-permute-start(bf16[64,2048]{1,0:T(8,128)(2,1)S(1)} %pad_maximum_fusion.refs_2_), channel_id=1, source_target_pairs={{0,2},{1,3},{2,4},{3,5},{4,6},{5,7},{8,10},{9,11},{10,12},{11,13},... | collective-permute-start | bytes 786440 | tf_op jit(solution)/shard_map/ppermute | solution.py:131
  8.7 9.3 %collective-permute-start = (bf16[64,2048]{1,0:T(8,128)(2,1)S(1)}, bf16[64,2048]{1,0:T(8,128)(2,1)S(1)}, u32[]{:S(2)}, u32[]{:S(2)}) collective-permute-start(bf16[64,2048]{1,0:T(8,128)(2,1)S(1)} %pad_maximum_fusion.refs_2_), channel_id=1, source_target_pairs={{0,1},{1,0},{2,3},{3,2},{4,5},{5,4},{6,7},{7,6},{8,9},{9,8},{10,11... | collective-permute-start | bytes 786440 | tf_op jit(solution)/shard_map/ppermute | solution.py:134
  11.2 8.8 %collective-permute-start.9 = (bf16[64,2048]{1,0:T(8,128)(2,1)S(1)}, bf16[64,2048]{1,0:T(8,128)(2,1)S(1)}, u32[]{:S(2)}, u32[]{:S(2)}) collective-permute-start(bf16[64,2048]{1,0:T(8,128)(2,1)S(1)} %collective-permute-done.1.refs_4_), channel_id=1, source_target_pairs={{4,8},{5,9},{20,24},{21,25}} | collective-permute-start | bytes 786440 | tf_op jit(solution)/shard_map/ppermute | solution.py:131
  12.5 10.4 %collective-permute-start.7 = (bf16[64,2048]{1,0:T(8,128)(2,1)S(1)}, bf16[64,2048]{1,0:T(8,128)(2,1)S(1)}, u32[]{:S(2)}, u32[]{:S(2)}) collective-permute-start(bf16[64,2048]{1,0:T(8,128)(2,1)S(1)} %collective-permute-done.1.refs_4_), channel_id=1, source_target_pairs={{6,8},{7,9},{22,24},{23,25}} | collective-permute-start | bytes 786440 | tf_op jit(solution)/shard_map/ppermute | solution.py:131
  15.7 7.5 %collective-permute-start.2 = (bf16[64,2048]{1,0:T(8,128)(2,1)S(1)}, bf16[64,2048]{1,0:T(8,128)(2,1)S(1)}, u32[]{:S(2)}, u32[]{:S(2)}) collective-permute-start(bf16[64,2048]{1,0:T(8,128)(2,1)S(1)} %collective-permute-done.1.refs_4_), channel_id=1, source_target_pairs={{0,1},{1,0},{2,3},{3,2},{4,5},{5,4},{6,7},{7,6},{8,9},{9,8},{10,11... | collective-permute-start | bytes 786440 | tf_op jit(solution)/shard_map/ppermute | solution.py:134
  17.9 5.2 %collective-permute-start.6 = (bf16[64,2048]{1,0:T(8,128)(2,1)S(1)}, bf16[64,2048]{1,0:T(8,128)(2,1)S(1)}, u32[]{:S(2)}, u32[]{:S(2)}) collective-permute-start(bf16[64,2048]{1,0:T(8,128)(2,1)S(1)} %collective-permute-done.5.refs_8_), channel_id=1, source_target_pairs={{0,1},{1,0},{2,3},{3,2},{4,5},{5,4},{6,7},{7,6},{8,9},{9,8},{10,11... | collective-permute-start | bytes 786440 | tf_op jit(solution)/shard_map/ppermute | solution.py:134
  17.9 5.2 %collective-permute-start.4 = (bf16[64,2048]{1,0:T(8,128)(2,1)S(1)}, bf16[64,2048]{1,0:T(8,128)(2,1)S(1)}, u32[]{:S(2)}, u32[]{:S(2)}) collective-permute-start(bf16[64,2048]{1,0:T(8,128)(2,1)S(1)} %collective-permute-done.3.refs_6_), channel_id=1, source_target_pairs={{0,1},{1,0},{2,3},{3,2},{4,5},{5,4},{6,7},{7,6},{8,9},{9,8},{10,11... | collective-permute-start | bytes 786440 | tf_op jit(solution)/shard_map/ppermute | solution.py:134
  20.0 3.2 %collective-permute-start.10 = (bf16[64,2048]{1,0:T(8,128)(2,1)S(1)}, bf16[64,2048]{1,0:T(8,128)(2,1)S(1)}, u32[]{:S(2)}, u32[]{:S(2)}) collective-permute-start(bf16[64,2048]{1,0:T(8,128)(2,1)S(1)} %collective-permute-done.9.refs_12_), channel_id=1, source_target_pairs={{0,1},{1,0},{2,3},{3,2},{4,5},{5,4},{6,7},{7,6},{8,9},{9,8},{10,11... | collective-permute-start | bytes 786440 | tf_op jit(solution)/shard_map/ppermute | solution.py:134
  22.9 1.5 %collective-permute-start.8 = (bf16[64,2048]{1,0:T(8,128)(2,1)S(1)}, bf16[64,2048]{1,0:T(8,128)(2,1)S(1)}, u32[]{:S(2)}, u32[]{:S(2)}) collective-permute-start(bf16[64,2048]{1,0:T(8,128)(2,1)S(1)} %collective-permute-done.7.refs_10_), channel_id=1, source_target_pairs={{0,1},{1,0},{2,3},{3,2},{4,5},{5,4},{6,7},{7,6},{8,9},{9,8},{10,11... | collective-permute-start | bytes 786440 | tf_op jit(solution)/shard_map/ppermute | solution.py:134
  24.5 1.2 %copy-start.1 = (bf16[1,64,8192]{2,1,0:T(8,128)(2,1)S(1)}, bf16[1,64,8192]{2,1,0:T(8,128)(2,1)}, u32[]{:S(2)}) copy-start(bf16[1,64,8192]{2,1,0:T(8,128)(2,1)} %param.4) | copy-start | bytes 3145732

commit v2 on v0

v2 whole, which is shorter than its diff:
```python
import functools
import math

import jax
import jax.numpy as jnp
from jax import lax
from jax.experimental import pallas as pl
from jax.experimental.pallas import tpu as pltpu
from jax.sharding import PartitionSpec as P

QH = 64
KVH = 8
HD = 128
GROUP = 8
WIDE = GROUP * HD
MASKED = -1e30
EXPONENT_SCALE = math.log2(math.e) / math.sqrt(HD)
LOW_TOTAL, HIGH_TOTAL = 2.0**-60, 2.0**80
VMEM_LIMIT = 24 * 1024 * 1024


def join_kernel(keys, values, joined, sems):
    copies = [
        pltpu.make_async_copy(keys, joined.at[:, : KVH * HD], sems.at[0]),
        pltpu.make_async_copy(values, joined.at[:, KVH * HD :], sems.at[1]),
    ]
    for copy in copies:
        copy.start()
    for copy in copies:
        copy.wait()


def doc_starts(lengths_row, positions):
    doc_ends = jnp.cumsum(lengths_row)
    return jnp.max(jnp.where(doc_ends[None, :] <= positions[:, None], doc_ends, 0), axis=1)


def columns(first, width=HD):
    return pl.ds(first if isinstance(first, int) else pl.multiple_of(first, HD), width)


def mask_of(first, rows, tokens, bases, first_position, starts):
    row_position = first_position + first + lax.broadcasted_iota(jnp.int32, (rows, tokens), 0)
    column = lax.broadcasted_iota(jnp.int32, (rows, tokens), 1)
    begin = starts[first : first + rows, :tokens]
    parts = []
    for base in bases:
        key_position = base + column
        allowed = (key_position >= begin) & (key_position <= row_position)
        parts.append(jnp.where(allowed, 0.0, MASKED))
    return jnp.concatenate(parts, axis=1)


def exponents_of(g, first, rows, q, blocks, mask):
    q_rows = jnp.concatenate(
        [q[first : first + rows, columns((g * GROUP + h) * HD)] for h in range(GROUP)], axis=0
    )
    k = jnp.concatenate([b[:, columns(g * HD)] for b in blocks], axis=0)
    scores = lax.dot_general(
        q_rows, k, (((1,), (1,)), ((), ())), preferred_element_type=jnp.float32
    )
    masked = scores.reshape(GROUP, rows, -1) + mask[None]
    return masked.reshape(scores.shape) * EXPONENT_SCALE


def weighted_sum(g, exponents, blocks):
    v = jnp.concatenate([b[:, columns((KVH + g) * HD)] for b in blocks], axis=0)
    v = jnp.concatenate([v, jnp.ones_like(v)], axis=1)
    weights = jnp.exp2(exponents).astype(jnp.bfloat16)
    return jnp.dot(weights, v, preferred_element_type=jnp.float32)


def load_kernel(source, target, sem):
    copy = pltpu.make_async_copy(source, target, sem)
    copy.start()
    copy.wait()


def early_kernel(base_of, q, starts, *refs):
    blocks, summed = refs[:-1], refs[-1]
    tokens = q.shape[0]
    index = lax.axis_index("seq")
    mask = mask_of(0, tokens, tokens, base_of(index, tokens), index * tokens, starts)
    for g in range(KVH):
        summed[g] = weighted_sum(g, exponents_of(g, 0, tokens, q, blocks, mask), blocks)


def late_kernel(group, base_of, late_base_of, q, starts, summed, early, high, middle, out_hbm, out, sems):
    tokens = q.shape[0]
    index = lax.axis_index("seq")
    early_bases = base_of(index, tokens)
    at_high, at_middle = late_base_of(index, tokens)

    def store(g, first, rows, total):
        result = (total[:, :HD] / total[:, HD:]).astype(jnp.bfloat16)
        for h in range(GROUP):
            out[first : first + rows, columns((g * GROUP + h) * HD)] = result[
                h * rows : (h + 1) * rows
            ]

    def copy_of(g):
        part = columns(g * WIDE, WIDE)
        return pltpu.make_async_copy(out.at[:, part], out_hbm.at[:, part], sems.at[g])

    def earlier(g, first, rows):
        return jnp.concatenate(
            [summed[g, h * tokens + first : h * tokens + first + rows] for h in range(GROUP)],
            axis=0,
        )

    def shifted(first, rows, blocks, bases):
        mask = mask_of(first, rows, tokens, bases, index * tokens, starts)

        def one(g, _):
            exponents = exponents_of(g, first, rows, q, blocks, mask)
            peak = jnp.max(exponents, axis=1, keepdims=True)
            store(g, first, rows, weighted_sum(g, exponents - peak, blocks))
            return 0

        lax.fori_loop(0, KVH, one, 0)

    def finish(rows, blocks, bases):
        mask = mask_of(0, rows, tokens, bases, index * tokens, starts)
        faults = jnp.zeros((GROUP * tokens, HD), jnp.float32)
        for g in range(KVH):
            new = weighted_sum(g, exponents_of(g, 0, rows, q, blocks, mask), blocks)
            totals = [earlier(g, 0, rows) + new]
            if rows < tokens:
                totals.append(earlier(g, rows, tokens - rows))
            for first, total in zip((0, rows), totals):
                store(g, first, total.shape[0] // GROUP, total)
            weights = jnp.concatenate([total[:, HD:] for total in totals], axis=0)
            sound = (weights > LOW_TOTAL) & (weights < HIGH_TOTAL)
            faults = jnp.maximum(faults, jnp.where(sound, 0.0, 1.0))
            copy_of(g).start()
        any_fault = jnp.max(faults) > 0.0
        for g in range(KVH):
            copy_of(g).wait()

        @pl.when(any_fault)
        def _():
            shifted(0, rows, early + blocks, early_bases + bases)
            if rows < tokens:
                shifted(rows, tokens - rows, early, early_bases)
            for g in range(KVH):
                copy_of(g).start()
            for g in range(KVH):
                copy_of(g).wait()

    is_middle = index // 2 == group
    pl.when(~is_middle)(functools.partial(finish, tokens, high, at_high))
    pl.when(is_middle)(functools.partial(finish, tokens // 2, middle, at_middle))


def closed(routes, count):
    onward = dict(routes)
    backward = {b: a for a, b in routes}
    for device in range(count):
        sibling = device ^ 1
        if device not in onward and device not in backward and sibling not in backward:
            onward[device], backward[sibling] = sibling, device
    for device in range(count):
        if device not in onward:
            start = device
            while start in backward:
                start = backward[start]
            onward[device], backward[start] = start, device
    return sorted(onward.items())


def per_device(queries, keys, values, doc_lengths):
    tokens = queries.shape[1]
    seq_count = lax.axis_size("seq")
    pairs = seq_count // 2
    group = pairs // 2
    half = group // 2
    never = 1 << 30

    def send(block, routes):
        devices = [(2 * a + i, 2 * b + j) for a, i, b, j in routes]
        return lax.ppermute(block, "seq", closed(devices, seq_count))

    def swap(block):
        return lax.ppermute(block, "seq", [(2 * c + i, 2 * c + 1 - i) for c in range(pairs) for i in (0, 1)])

    any_spec = pl.BlockSpec(memory_space=pl.ANY)
    vmem_spec = pl.BlockSpec(memory_space=pltpu.VMEM)
    params = pltpu.CompilerParams(vmem_limit_bytes=VMEM_LIMIT)

    def in_hbm(array):
        return pltpu.with_memory_space_constraint(array, pltpu.HBM)

    def resident(array):
        return pltpu.with_memory_space_constraint(array, pltpu.VMEM)

    own = pl.pallas_call(
        join_kernel,
        out_shape=pltpu.VMEM((tokens, 2 * KVH * HD), jnp.bfloat16),
        in_specs=[any_spec] * 2,
        out_specs=vmem_spec,
        scratch_shapes=[pltpu.SemaphoreType.DMA((2,))],
        compiler_params=params,
    )(in_hbm(keys[0]), in_hbm(values[0]))

    halves = [(first, first + half) for first in range(0, pairs, half)]
    up = [(c, c + half) for c in [*range(half + 1), *range(group, group + half)]]
    along = {
        d: [(c - d, c) for lo, hi in halves for c in range(lo + d, hi)] + [(group - d, group)]
        for d in range(1, half)
    }
    routes = {half: up, **along}
    ordered = [half, *along]
    distances = [ordered, [ordered[1], half, *ordered[2:]]]
    up_round = [0, 1]
    first = []
    for of_zero, of_one in zip(*distances):
        both = ((0, of_zero), (1, of_one))
        first.append(send(own, [(a, core, b, core) for core, d in both for a, b in routes[d]]))
    sibling = swap(own)
    own_later, _ = lax.optimization_barrier((own, first[1]))
    cross = [
        send(
            own_later,
            [
                (lo + (j - step) % half, core, lo + half + j, core)
                for lo in (0, group)
                for j in range(half)
                for core in (0, 1)
            ]
            + [
                (lo + half + j, core, lo + j, core)
                for lo in (0, group)
                for j in range(half)
                for core in (0, 1)
            ],
        )
        for step in range(1, half)
    ]
    far, far_blocks = [], []
    for low in range(0, half, 2):
        for core in (0, 1):
            one, two, other = half + low, half + low + 1, 1 - core
            passed = [(one, core, group, 0), (group, 0, one, other), (one, other, one, core)]
            passed += [(two, core, group, 1), (group, 1, group + 1, 0)]
            passed += [(group + 1, 0, group + 1, 1), (group + 1, 1, two, other)]
            passed += [(two, other, two, core)]
            far.append(send(first[up_round[core]], passed))
            far_blocks.append((low, core))

    def position(source, core, tokens, valid):
        return jnp.where(valid, (2 * source + core) * tokens, never)

    def early_bases(index, tokens):
        pair, core = index // 2, index % 2
        bases = [position(pair, core, tokens, True), position(pair, 1 - core, tokens, True)]
        for of_zero, of_one in zip(*distances):
            for other in (core, 1 - core):
                d = jnp.where(other == 0, of_zero, of_one)
                high = pair // half % 2 == 1
                valid = jnp.where(d == half, high, pair % half >= d) | (pair == group)
                bases.append(position(pair - d, other, tokens, valid))
        return bases

    def late_bases(index, tokens):
        pair, core = index // 2, index % 2
        local = pair % half
        at_high, at_middle = [], []
        for step in range(1, half):
            source = pair - half - local + (local + half - step) % half
            for other in (core, 1 - core):
                at_high.append(position(source, other, tokens, pair // half % 2 == 1))
        for low, other in far_blocks:
            at_middle.append(position(low + core, other, tokens, True))
            at_middle.append(position(low + 1 - core, other, tokens, True))
        return at_high, at_middle

    lengths_row = lax.dynamic_index_in_dim(doc_lengths, lax.axis_index("dp"), 0, keepdims=False)
    positions = lax.axis_index("seq") * tokens + jnp.arange(tokens, dtype=jnp.int32)
    starts = jnp.broadcast_to(doc_starts(lengths_row, positions)[:, None], (tokens, HD))
    early = [own, sibling]
    for block in first:
        early += [block, swap(block)]
    early = [resident(a) for a in early]
    q = pl.pallas_call(
        load_kernel,
        out_shape=pltpu.VMEM((tokens, QH * HD), jnp.bfloat16),
        in_specs=[any_spec],
        out_specs=vmem_spec,
        scratch_shapes=[pltpu.SemaphoreType.DMA(())],
        compiler_params=params,
    )(in_hbm(queries[0]))
    summed = pl.pallas_call(
        functools.partial(early_kernel, early_bases),
        out_shape=pltpu.VMEM((KVH, GROUP * tokens, 2 * HD), jnp.float32),
        in_specs=[vmem_spec] * (2 + len(early)),
        out_specs=vmem_spec,
        compiler_params=params,
        cost_estimate=pl.CostEstimate(flops=1, bytes_accessed=1, transcendentals=0),
    )(resident(q), resident(starts), *early)

    late = []
    for blocks in (cross, far):
        held = []
        for block in blocks:
            block, summed = lax.optimization_barrier((block, summed))
            held += [block, swap(block)]
        late.append([resident(a) for a in held])
    out = pl.pallas_call(
        functools.partial(late_kernel, group, early_bases, late_bases),
        out_shape=jax.ShapeDtypeStruct((tokens, QH * HD), jnp.bfloat16),
        in_specs=[vmem_spec] * 3 + [[vmem_spec] * len(a) for a in (early, *late)],
        out_specs=any_spec,
        scratch_shapes=[
            pltpu.VMEM((tokens, QH * HD), jnp.bfloat16),
            pltpu.SemaphoreType.DMA((KVH,)),
        ],
        compiler_params=params,
    )(resident(q), resident(starts), resident(summed), early, *late)
    return out[None]


def solution(mesh):
    placed = (P("dp", "seq", None), P("dp", "seq", None), P("dp", "seq", None), P())
    return jax.shard_map(
        per_device, mesh=mesh, in_specs=placed, out_specs=P("dp", "seq", None), check_vma=False
    )
```

time: 142 us -> 37.8 us (0.27)
  the two profiles are of different devices: /device:TPU:16 before, /device:TPU:17 now
where the time goes in v2:
time: 37.8 us; the launch traced here: 37.6 us
  Pallas kernels  17.4 us (46%)
  waiting for transfers between devices  12.5 us (33%)
  starting transfers between devices  6.79 us (18%)
  other arithmetic  0.6 us (2%)
    pallas_call x1, Pallas kernels, per_device(): pl.pallas_call(functools.partial(late_kernel, group, early_bases, late_ba...  13 us
    ppermute x5, waiting for transfers between devices, send(): return lax.ppermute(block, 'seq', closed(devices, seq_count))  10.7 us
    ppermute x5, starting transfers between devices, send(): return lax.ppermute(block, 'seq', closed(devices, seq_count))  4.84 us
    pallas_call x1, Pallas kernels, per_device(): pl.pallas_call(functools.partial(early_kernel, early_bases), out_shape=pl...  2.11 us
    ppermute x6, starting transfers between devices, swap(): lax.ppermute(block, 'seq', [(2 * c + i, 2 * c + 1 - i) for c in range(pai...  1.95 us
    ppermute x6, waiting for transfers between devices, swap(): lax.ppermute(block, 'seq', [(2 * c + i, 2 * c + 1 - i) for c in range(pai...  1.78 us
    pallas_call x1, Pallas kernels, per_device(): pl.pallas_call(load_kernel, out_shape=pltpu.VMEM((tokens, QH * HD), jnp.b...  1.23 us
    pallas_call x1, Pallas kernels, per_device(): pl.pallas_call(join_kernel, out_shape=pltpu.VMEM((tokens, 2 * KVH * HD),...  1 us
  transfers between devices with their start and end apart: 11, of which 6 were waited for; matrix products, arithmetic and copies ran while one was open for 2% of the time, Pallas kernels for 9%

profile of v2, /device:TPU:17, one launch (start us, length us, event | category | flops | bytes accessed | tf_op | source)
XLA Modules:
  0.0 37.6 jit_solution(10315616451062003478)
XLA Ops:
  0.0 1.0 %shard_map.47.refs_0_.early_0_ = bf16[64,2048]{1,0:T(8,128)(2,1)S(1)} custom-call(bf16[64,1024]{1,0:T(8,128)(2,1)} %bitcast.11, bf16[64,1024]{1,0:T(8,128)(2,1)} %bitcast.12), custom_call_target="tpu_custom_call" | custom-call | tf_op jit(solution)/shard_map/pallas_call | solution.py:196
  1.0 0.7 %collective-permute-start.5 = (bf16[64,2048]{1,0:T(8,128)(2,1)S(1)}, bf16[64,2048]{1,0:T(8,128)(2,1)S(1)}, u32[]{:S(2)}, u32[]{:S(2)}) collective-permute-start(bf16[64,2048]{1,0:T(8,128)(2,1)S(1)} %shard_map.47.refs_0_.early_0_), channel_id=1, source_target_pairs={{0,1},{1,0},{2,3},{3,2},{4,5},{5,4},{6,7},{7,6},{8,9},{9,8},{10,11... | collective-permute-start | bytes 786440 | tf_op jit(solution)/shard_map/ppermute | solution.py:184
  1.7 1.2 %collective-permute-start.2 = (bf16[64,2048]{1,0:T(8,128)(2,1)S(1)}, bf16[64,2048]{1,0:T(8,128)(2,1)S(1)}, u32[]{:S(2)}, u32[]{:S(2)}) collective-permute-start(bf16[64,2048]{1,0:T(8,128)(2,1)S(1)} %shard_map.47.refs_0_.early_0_), channel_id=1, source_target_pairs={{0,4},{1,3},{2,6},{3,1},{4,8},{5,7},{6,2},{7,9},{8,12},{9,11},{10,... | collective-permute-start | bytes 786440 | tf_op jit(solution)/shard_map/ppermute | solution.py:181
  3.0 1.3 %collective-permute-start = (bf16[64,2048]{1,0:T(8,128)(2,1)S(1)}, bf16[64,2048]{1,0:T(8,128)(2,1)S(1)}, u32[]{:S(2)}, u32[]{:S(2)}) collective-permute-start(bf16[64,2048]{1,0:T(8,128)(2,1)S(1)} %shard_map.47.refs_0_.early_0_), channel_id=1, source_target_pairs={{0,2},{1,5},{2,0},{3,7},{4,6},{5,9},{6,8},{7,3},{8,10},{9,13},{10,... | collective-permute-start | bytes 786440 | tf_op jit(solution)/shard_map/ppermute | solution.py:181
  4.3 0.3 reduce-window.9
  4.6 0.1 slice.10
  4.7 0.1 slice_reduce_fusion
  4.8 5.8 %collective-permute-done.refs_4_.early_4_ = bf16[64,2048]{1,0:T(8,128)(2,1)S(1)} collective-permute-done((bf16[64,2048]{1,0:T(8,128)(2,1)S(1)}, bf16[64,2048]{1,0:T(8,128)(2,1)S(1)}, u32[]{:S(2)}, u32[]{:S(2)}) %collective-permute-start) | collective-permute-done | bytes 262176 | tf_op jit(solution)/shard_map/ppermute | solution.py:181
  10.6 1.7 %collective-permute-start.4 = (bf16[64,2048]{1,0:T(8,128)(2,1)S(1)}, bf16[64,2048]{1,0:T(8,128)(2,1)S(1)}, u32[]{:S(2)}, u32[]{:S(2)}) collective-permute-start(bf16[64,2048]{1,0:T(8,128)(2,1)S(1)} %shard_map.47.refs_0_.early_0_), channel_id=1, source_target_pairs={{0,6},{1,7},{2,4},{3,5},{4,0},{5,1},{6,2},{7,3},{8,14},{9,15},{10,... | collective-permute-start | bytes 786440 | tf_op jit(solution)/shard_map/ppermute | solution.py:181
  12.3 0.7 %collective-permute-start.6 = (bf16[64,2048]{1,0:T(8,128)(2,1)S(1)}, bf16[64,2048]{1,0:T(8,128)(2,1)S(1)}, u32[]{:S(2)}, u32[]{:S(2)}) collective-permute-start(bf16[64,2048]{1,0:T(8,128)(2,1)S(1)} %collective-permute-done.2.refs_2_.early_2_), channel_id=1, source_target_pairs={{0,1},{1,0},{2,3},{3,2},{4,5},{5,4},{6,7},{7,6},{8,9},{9,8},{10,11... | collective-permute-start | bytes 786440 | tf_op jit(solution)/shard_map/ppermute | solution.py:184
  13.0 0.2 collective-permute-start.3
  13.2 0.4 %collective-permute-start.1 = (bf16[64,2048]{1,0:T(8,128)(2,1)S(1)}, bf16[64,2048]{1,0:T(8,128)(2,1)S(1)}, u32[]{:S(2)}, u32[]{:S(2)}) collective-permute-start(bf16[64,2048]{1,0:T(8,128)(2,1)S(1)} %collective-permute-done.refs_4_.early_4_), channel_id=1, source_target_pairs={{0,1},{1,0},{2,3},{3,2},{4,5},{5,8},{6,7},{7,9},{8,4},{9,10},{10,1... | collective-permute-start | bytes 786440 | tf_op jit(solution)/shard_map/ppermute | solution.py:181
  13.6 0.1 add_bitcast_fusion
  13.7 1.2 %shard_map.46.q = bf16[64,8192]{1,0:T(8,128)(2,1)S(1)} custom-call(bf16[64,8192]{1,0:T(8,128)(2,1)} %bitcast.10), custom_call_target="tpu_custom_call" | custom-call | tf_op jit(solution)/shard_map/pallas_call | solution.py:284
  15.0 0.2 select_reduce_fusion
  15.2 0.1 broadcast_in_dim.18.starts
  15.2 2.1 %shard_map.48.summed = f32[8,512,256]{2,1,0:T(8,128)S(1)} custom-call(bf16[64,8192]{1,0:T(8,128)(2,1)S(1)} %shard_map.46.q, s32[64,128]{1,0:T(8,128)S(1)} %broadcast_in_dim.18.starts, bf16[64,2048]{1,0:T(8,128)(2,1)S(1)} %shard_map.47.refs_0_.early_0_, bf16[64,2048]{1,0:T(8,128)(2,1)S(1)} %collective-permute-done.5.refs_1_.early_1_, ...), custom_call_target="tpu_custom_call" | custom-call | flops 1 | bytes 1 | tf_op jit(solution)/shard_map/pallas_call | solution.py:292
  17.4 0.3 collective-permute-done.4.high_0_
  17.7 4.6 %collective-permute-done.3.middle_0_ = bf16[64,2048]{1,0:T(8,128)(2,1)S(1)} collective-permute-done((bf16[64,2048]{1,0:T(8,128)(2,1)S(1)}, bf16[64,2048]{1,0:T(8,128)(2,1)S(1)}, u32[]{:S(2)}, u32[]{:S(2)}) %collective-permute-start.3) | collective-permute-done | bytes 262176 | tf_op jit(solution)/shard_map/ppermute | solution.py:181
  22.3 0.5 %collective-permute-start.9 = (bf16[64,2048]{1,0:T(8,128)(2,1)S(1)}, bf16[64,2048]{1,0:T(8,128)(2,1)S(1)}, u32[]{:S(2)}, u32[]{:S(2)}) collective-permute-start(bf16[64,2048]{1,0:T(8,128)(2,1)S(1)} %collective-permute-done.3.middle_0_), channel_id=1, source_target_pairs={{0,1},{1,0},{2,3},{3,2},{4,5},{5,4},{6,7},{7,6},{8,9},{9,8},{10,11... | collective-permute-start | bytes 786440 | tf_op jit(solution)/shard_map/ppermute | solution.py:184
  22.8 1.0 %collective-permute-done.10.middle_3_ = bf16[64,2048]{1,0:T(8,128)(2,1)S(1)} collective-permute-done((bf16[64,2048]{1,0:T(8,128)(2,1)S(1)}, bf16[64,2048]{1,0:T(8,128)(2,1)S(1)}, u32[]{:S(2)}, u32[]{:S(2)}) %collective-permute-start.10) | collective-permute-done | bytes 262176 | tf_op jit(solution)/shard_map/ppermute | solution.py:184
  23.9 0.4 collective-permute-done.9.middle_1_
  24.2 0.4 collective-permute-done.8.high_1_
  24.6 13.0 %shard_map.49 = bf16[64,8192]{1,0:T(8,128)(2,1)} custom-call(bf16[64,8192]{1,0:T(8,128)(2,1)S(1)} %shard_map.46.q, s32[64,128]{1,0:T(8,128)S(1)} %broadcast_in_dim.18.starts, f32[8,512,256]{2,1,0:T(8,128)S(1)} %shard_map.48.summed, bf16[64,2048]{1,0:T(8,128)(2,1)S(1)} %shard_map.47.refs_0_.early_0_, ...), custom_call_target="tpu_custom_call" | custom-call | tf_op jit(solution)/shard_map/pallas_call | solution.py:308
  (14 shorter events, 0.1 us)
Async XLA Ops:
  0.0 4.3 %copy-start = (s32[2,129]{1,0:T(2,128)S(1)}, s32[2,129]{1,0:T(2,128)}, u32[]{:S(2)}) copy-start(s32[2,129]{1,0:T(2,128)} %param.7) | copy-start | bytes 3100
  1.0 12.2 %collective-permute-start.5 = (bf16[64,2048]{1,0:T(8,128)(2,1)S(1)}, bf16[64,2048]{1,0:T(8,128)(2,1)S(1)}, u32[]{:S(2)}, u32[]{:S(2)}) collective-permute-start(bf16[64,2048]{1,0:T(8,128)(2,1)S(1)} %shard_map.47.refs_0_.early_0_), channel_id=1, source_target_pairs={{0,1},{1,0},{2,3},{3,2},{4,5},{5,4},{6,7},{7,6},{8,9},{9,8},{10,11... | collective-permute-start | bytes 786440 | tf_op jit(solution)/shard_map/ppermute | solution.py:184
  1.7 10.5 %collective-permute-start.2 = (bf16[64,2048]{1,0:T(8,128)(2,1)S(1)}, bf16[64,2048]{1,0:T(8,128)(2,1)S(1)}, u32[]{:S(2)}, u32[]{:S(2)}) collective-permute-start(bf16[64,2048]{1,0:T(8,128)(2,1)S(1)} %shard_map.47.refs_0_.early_0_), channel_id=1, source_target_pairs={{0,4},{1,3},{2,6},{3,1},{4,8},{5,7},{6,2},{7,9},{8,12},{9,11},{10,... | collective-permute-start | bytes 786440 | tf_op jit(solution)/shard_map/ppermute | solution.py:181
  3.0 7.6 %collective-permute-start = (bf16[64,2048]{1,0:T(8,128)(2,1)S(1)}, bf16[64,2048]{1,0:T(8,128)(2,1)S(1)}, u32[]{:S(2)}, u32[]{:S(2)}) collective-permute-start(bf16[64,2048]{1,0:T(8,128)(2,1)S(1)} %shard_map.47.refs_0_.early_0_), channel_id=1, source_target_pairs={{0,2},{1,5},{2,0},{3,7},{4,6},{5,9},{6,8},{7,3},{8,10},{9,13},{10,... | collective-permute-start | bytes 786440 | tf_op jit(solution)/shard_map/ppermute | solution.py:181
  10.6 7.1 %collective-permute-start.4 = (bf16[64,2048]{1,0:T(8,128)(2,1)S(1)}, bf16[64,2048]{1,0:T(8,128)(2,1)S(1)}, u32[]{:S(2)}, u32[]{:S(2)}) collective-permute-start(bf16[64,2048]{1,0:T(8,128)(2,1)S(1)} %shard_map.47.refs_0_.early_0_), channel_id=1, source_target_pairs={{0,6},{1,7},{2,4},{3,5},{4,0},{5,1},{6,2},{7,3},{8,14},{9,15},{10,... | collective-permute-start | bytes 786440 | tf_op jit(solution)/shard_map/ppermute | solution.py:181
  12.3 2.9 %collective-permute-start.6 = (bf16[64,2048]{1,0:T(8,128)(2,1)S(1)}, bf16[64,2048]{1,0:T(8,128)(2,1)S(1)}, u32[]{:S(2)}, u32[]{:S(2)}) collective-permute-start(bf16[64,2048]{1,0:T(8,128)(2,1)S(1)} %collective-permute-done.2.refs_2_.early_2_), channel_id=1, source_target_pairs={{0,1},{1,0},{2,3},{3,2},{4,5},{5,4},{6,7},{7,6},{8,9},{9,8},{10,11... | collective-permute-start | bytes 786440 | tf_op jit(solution)/shard_map/ppermute | solution.py:184
  13.0 9.3 %collective-permute-start.3 = (bf16[64,2048]{1,0:T(8,128)(2,1)S(1)}, bf16[64,2048]{1,0:T(8,128)(2,1)S(1)}, u32[]{:S(2)}, u32[]{:S(2)}) collective-permute-start(bf16[64,2048]{1,0:T(8,128)(2,1)S(1)} %collective-permute-done.2.refs_2_.early_2_), channel_id=1, source_target_pairs={{0,1},{1,0},{2,3},{3,2},{4,8},{5,4},{6,9},{7,6},{8,5},{9,10},{10,1... | collective-permute-start | bytes 786440 | tf_op jit(solution)/shard_map/ppermute | solution.py:181
  13.2 2.0 %collective-permute-start.7 = (bf16[64,2048]{1,0:T(8,128)(2,1)S(1)}, bf16[64,2048]{1,0:T(8,128)(2,1)S(1)}, u32[]{:S(2)}, u32[]{:S(2)}) collective-permute-start(bf16[64,2048]{1,0:T(8,128)(2,1)S(1)} %collective-permute-done.refs_4_.early_4_), channel_id=1, source_target_pairs={{0,1},{1,0},{2,3},{3,2},{4,5},{5,4},{6,7},{7,6},{8,9},{9,8},{10,11... | collective-permute-start | bytes 786440 | tf_op jit(solution)/shard_map/ppermute | solution.py:184
  13.2 9.1 %collective-permute-start.1 = (bf16[64,2048]{1,0:T(8,128)(2,1)S(1)}, bf16[64,2048]{1,0:T(8,128)(2,1)S(1)}, u32[]{:S(2)}, u32[]{:S(2)}) collective-permute-start(bf16[64,2048]{1,0:T(8,128)(2,1)S(1)} %collective-permute-done.refs_4_.early_4_), channel_id=1, source_target_pairs={{0,1},{1,0},{2,3},{3,2},{4,5},{5,8},{6,7},{7,9},{8,4},{9,10},{10,1... | collective-permute-start | bytes 786440 | tf_op jit(solution)/shard_map/ppermute | solution.py:181
  22.3 1.5 %collective-permute-start.10 = (bf16[64,2048]{1,0:T(8,128)(2,1)S(1)}, bf16[64,2048]{1,0:T(8,128)(2,1)S(1)}, u32[]{:S(2)}, u32[]{:S(2)}) collective-permute-start(bf16[64,2048]{1,0:T(8,128)(2,1)S(1)} %collective-permute-done.1.middle_2_), channel_id=1, source_target_pairs={{0,1},{1,0},{2,3},{3,2},{4,5},{5,4},{6,7},{7,6},{8,9},{9,8},{10,11... | collective-permute-start | bytes 786440 | tf_op jit(solution)/shard_map/ppermute | solution.py:184
  22.3 1.9 %collective-permute-start.9 = (bf16[64,2048]{1,0:T(8,128)(2,1)S(1)}, bf16[64,2048]{1,0:T(8,128)(2,1)S(1)}, u32[]{:S(2)}, u32[]{:S(2)}) collective-permute-start(bf16[64,2048]{1,0:T(8,128)(2,1)S(1)} %collective-permute-done.3.middle_0_), channel_id=1, source_target_pairs={{0,1},{1,0},{2,3},{3,2},{4,5},{5,4},{6,7},{7,6},{8,9},{9,8},{10,11... | collective-permute-start | bytes 786440 | tf_op jit(solution)/shard_map/ppermute | solution.py:184
  22.8 1.8 %collective-permute-start.8 = (bf16[64,2048]{1,0:T(8,128)(2,1)S(1)}, bf16[64,2048]{1,0:T(8,128)(2,1)S(1)}, u32[]{:S(2)}, u32[]{:S(2)}) collective-permute-start(bf16[64,2048]{1,0:T(8,128)(2,1)S(1)} %collective-permute-done.4.high_0_), channel_id=1, source_target_pairs={{0,1},{1,0},{2,3},{3,2},{4,5},{5,4},{6,7},{7,6},{8,9},{9,8},{10,11... | collective-permute-start | bytes 786440 | tf_op jit(solution)/shard_map/ppermute | solution.py:184

commit v3 on v2

v3 whole, which is shorter than its diff:
```python
import functools
import math

import jax
import jax.numpy as jnp
from jax import lax
from jax.experimental import pallas as pl
from jax.experimental.pallas import tpu as pltpu
from jax.sharding import PartitionSpec as P

QH = 64
KVH = 8
HD = 128
GROUP = 8
WIDE = GROUP * HD
MASKED = -1e30
EXPONENT_SCALE = math.log2(math.e) / math.sqrt(HD)
LOW_TOTAL, HIGH_TOTAL = 2.0**-60, 2.0**80
VMEM_LIMIT = 24 * 1024 * 1024


def join_kernel(keys, values, joined, sems):
    copies = [
        pltpu.make_async_copy(keys, joined.at[:, : KVH * HD], sems.at[0]),
        pltpu.make_async_copy(values, joined.at[:, KVH * HD :], sems.at[1]),
    ]
    for copy in copies:
        copy.start()
    for copy in copies:
        copy.wait()


def doc_starts(lengths_row, positions):
    doc_ends = jnp.cumsum(lengths_row)
    return jnp.max(jnp.where(doc_ends[None, :] <= positions[:, None], doc_ends, 0), axis=1)


def columns(first, width=HD):
    return pl.ds(first if isinstance(first, int) else pl.multiple_of(first, HD), width)


def mask_of(first, rows, tokens, bases, first_position, starts):
    row_position = first_position + first + lax.broadcasted_iota(jnp.int32, (rows, tokens), 0)
    column = lax.broadcasted_iota(jnp.int32, (rows, tokens), 1)
    begin = starts[first : first + rows, :tokens]
    parts = []
    for base in bases:
        key_position = base + column
        allowed = (key_position >= begin) & (key_position <= row_position)
        parts.append(jnp.where(allowed, 0.0, MASKED))
    return jnp.concatenate(parts, axis=1)


def exponents_of(g, first, rows, q, blocks, mask):
    q_rows = jnp.concatenate(
        [q[first : first + rows, columns((g * GROUP + h) * HD)] for h in range(GROUP)], axis=0
    )
    k = jnp.concatenate([b[:, columns(g * HD)] for b in blocks], axis=0)
    scores = lax.dot_general(
        q_rows, k, (((1,), (1,)), ((), ())), preferred_element_type=jnp.float32
    )
    masked = scores.reshape(GROUP, rows, -1) + mask[None]
    return masked.reshape(scores.shape) * EXPONENT_SCALE


def weighted_sum(g, exponents, blocks):
    v = jnp.concatenate([b[:, columns((KVH + g) * HD)] for b in blocks], axis=0)
    v = jnp.concatenate([v, jnp.ones_like(v)], axis=1)
    weights = jnp.exp2(exponents).astype(jnp.bfloat16)
    return jnp.dot(weights, v, preferred_element_type=jnp.float32)


def load_kernel(source, target, sem):
    copy = pltpu.make_async_copy(source, target, sem)
    copy.start()
    copy.wait()


def copy_out(g, out, out_hbm, sems):
    part = columns(g * WIDE, WIDE)
    return pltpu.make_async_copy(out.at[:, part], out_hbm.at[:, part], sems.at[g])


def store(g, first, total, out):
    rows = total.shape[0] // GROUP
    result = (total[:, :HD] / total[:, HD:]).astype(jnp.bfloat16)
    for h in range(GROUP):
        out[first : first + rows, columns((g * GROUP + h) * HD)] = result[h * rows : (h + 1) * rows]


def finish(totals_of, spans, q, starts, first_position, out, out_hbm, sems):
    tokens = q.shape[0]
    faults = jnp.zeros((GROUP * tokens, HD), jnp.float32)
    for g in range(KVH):
        totals = totals_of(g)
        for (first, *_), total in zip(spans, totals):
            store(g, first, total, out)
        weights = jnp.concatenate([total[:, HD:] for total in totals], axis=0)
        sound = (weights > LOW_TOTAL) & (weights < HIGH_TOTAL)
        faults = jnp.maximum(faults, jnp.where(sound, 0.0, 1.0))
        copy_out(g, out, out_hbm, sems).start()
    any_fault = jnp.max(faults) > 0.0
    for g in range(KVH):
        copy_out(g, out, out_hbm, sems).wait()

    @pl.when(any_fault)
    def _():
        for first, rows, blocks, bases in spans:
            mask = mask_of(first, rows, tokens, bases, first_position, starts)

            def one(g, _):
                exponents = exponents_of(g, first, rows, q, blocks, mask)
                peak = jnp.max(exponents, axis=1, keepdims=True)
                store(g, first, weighted_sum(g, exponents - peak, blocks), out)
                return 0

            lax.fori_loop(0, KVH, one, 0)
        for g in range(KVH):
            copy_out(g, out, out_hbm, sems).start()
        for g in range(KVH):
            copy_out(g, out, out_hbm, sems).wait()


def early_kernel(group, half, base_of, q, starts, *refs):
    blocks, (summed, out_hbm, out, sems) = refs[:-4], refs[-4:]
    tokens = q.shape[0]
    index = lax.axis_index("seq")
    bases = base_of(index, tokens)
    mask = mask_of(0, tokens, tokens, bases, index * tokens, starts)
    for g in range(KVH):
        summed[g] = weighted_sum(g, exponents_of(g, 0, tokens, q, blocks, mask), blocks)
    pair = index // 2

    @pl.when((pair != group) & (pair // half % 2 == 0))
    def _():
        spans = [(0, tokens, blocks, bases)]
        finish(lambda g: [summed[g]], spans, q, starts, index * tokens, out, out_hbm, sems)


def late_kernel(
    reads, rows, base_of, late_base_of, q, starts, summed, early, late, _, out_hbm, out, sems
):
    tokens = q.shape[0]
    index = lax.axis_index("seq")

    def earlier(g, first, length):
        return jnp.concatenate(
            [summed[g, h * tokens + first : h * tokens + first + length] for h in range(GROUP)],
            axis=0,
        )

    @pl.when(reads(index // 2))
    def _():
        early_bases, bases = base_of(index, tokens), late_base_of(index, tokens)
        mask = mask_of(0, rows, tokens, bases, index * tokens, starts)
        exponents = [exponents_of(g, 0, rows, q, late, mask) for g in range(KVH)]
        new = [weighted_sum(g, exponents[g], late) for g in range(KVH)]
        spans = [(0, rows, early + late, early_bases + bases)]
        if rows < tokens:
            spans.append((rows, tokens - rows, early, early_bases))

        def totals_of(g):
            rest = [earlier(g, first, length) for first, length, *_ in spans[1:]]
            return [earlier(g, 0, rows) + new[g], *rest]

        finish(totals_of, spans, q, starts, index * tokens, out, out_hbm, sems)


def closed(routes, count):
    onward = dict(routes)
    backward = {b: a for a, b in routes}
    for device in range(count):
        sibling = device ^ 1
        if device not in onward and device not in backward and sibling not in backward:
            onward[device], backward[sibling] = sibling, device
    for device in range(count):
        if device not in onward:
            start = device
            while start in backward:
                start = backward[start]
            onward[device], backward[start] = start, device
    return sorted(onward.items())


def per_device(queries, keys, values, doc_lengths):
    tokens = queries.shape[1]
    seq_count = lax.axis_size("seq")
    pairs = seq_count // 2
    group = pairs // 2
    half = group // 2
    never = 1 << 30

    def send(block, routes):
        devices = [(2 * a + i, 2 * b + j) for a, i, b, j in routes]
        return lax.ppermute(block, "seq", closed(devices, seq_count))

    def swap(block):
        return lax.ppermute(block, "seq", [(2 * c + i, 2 * c + 1 - i) for c in range(pairs) for i in (0, 1)])

    any_spec = pl.BlockSpec(memory_space=pl.ANY)
    vmem_spec = pl.BlockSpec(memory_space=pltpu.VMEM)
    params = pltpu.CompilerParams(vmem_limit_bytes=VMEM_LIMIT)

    def in_hbm(array):
        return pltpu.with_memory_space_constraint(array, pltpu.HBM)

    def resident(array):
        return pltpu.with_memory_space_constraint(array, pltpu.VMEM)

    own = pl.pallas_call(
        join_kernel,
        out_shape=pltpu.VMEM((tokens, 2 * KVH * HD), jnp.bfloat16),
        in_specs=[any_spec] * 2,
        out_specs=vmem_spec,
        scratch_shapes=[pltpu.SemaphoreType.DMA((2,))],
        compiler_params=params,
    )(in_hbm(keys[0]), in_hbm(values[0]))

    halves = [(first, first + half) for first in range(0, pairs, half)]
    up = [(c, c + half) for c in [*range(half + 1), *range(group, group + half)]]
    along = {
        d: [(c - d, c) for lo, hi in halves for c in range(lo + d, hi)] + [(group - d, group)]
        for d in range(1, half)
    }
    routes = {half: up, **along}
    distances = [half, *along]
    sibling = swap(own)
    own_next, _ = lax.optimization_barrier((own, sibling))
    first = [
        send(
            own if d == half else own_next,
            [(a, core, b, core) for a, b in routes[d] for core in (0, 1)],
        )
        for d in distances
    ]
    swapped = [swap(block) for block in first]
    q = pl.pallas_call(
        load_kernel,
        out_shape=pltpu.VMEM((tokens, QH * HD), jnp.bfloat16),
        in_specs=[any_spec],
        out_specs=vmem_spec,
        scratch_shapes=[pltpu.SemaphoreType.DMA(())],
        compiler_params=params,
    )(in_hbm(queries[0]))
    first[0], q = lax.optimization_barrier((first[0], q))
    own_later, _ = lax.optimization_barrier((own, first[0]))
    came_up = first[0]
    cross = [
        send(
            own_later,
            [
                (lo + (j - step) % half, core, lo + half + j, core)
                for lo in (0, group)
                for j in range(half)
                for core in (0, 1)
            ]
            + [
                (lo + half + j, core, lo + j, core)
                for lo in (0, group)
                for j in range(half)
                for core in (0, 1)
            ],
        )
        for step in range(1, half)
    ]
    far = []
    for j in range(half):
        back = [] if j % 2 == 0 else [group + 1]
        route = [half + j, group, *back, half + j]
        far.append(
            send(came_up, [(a, c, b, c) for a, b in zip(route, route[1:]) for c in (0, 1)])
        )

    def position(source, core, tokens, valid):
        return jnp.where(valid, (2 * source + core) * tokens, never)

    def early_bases(index, tokens):
        pair, core = index // 2, index % 2
        bases = [position(pair, core, tokens, True), position(pair, 1 - core, tokens, True)]
        for d in distances:
            reached = pair // half % 2 == 1 if d == half else pair % half >= d
            for other in (core, 1 - core):
                bases.append(position(pair - d, other, tokens, reached | (pair == group)))
        return bases

    def high_bases(index, tokens):
        pair, core = index // 2, index % 2
        local = pair % half
        bases = []
        for step in range(1, half):
            source = pair - half - local + (local + half - step) % half
            bases += [position(source, other, tokens, True) for other in (core, 1 - core)]
        return bases

    def middle_bases(index, tokens):
        core = index % 2
        return [
            position(low, other, tokens, True) for low in range(half) for other in (core, 1 - core)
        ]

    lengths_row = lax.dynamic_index_in_dim(doc_lengths, lax.axis_index("dp"), 0, keepdims=False)
    positions = lax.axis_index("seq") * tokens + jnp.arange(tokens, dtype=jnp.int32)
    starts = jnp.broadcast_to(doc_starts(lengths_row, positions)[:, None], (tokens, HD))
    early = [own, sibling]
    for block, other in zip(first, swapped):
        early += [block, other]
    early = [resident(a) for a in early]
    out_scratch = [pltpu.VMEM((tokens, QH * HD), jnp.bfloat16), pltpu.SemaphoreType.DMA((KVH,))]
    result = jax.ShapeDtypeStruct((tokens, QH * HD), jnp.bfloat16)
    summed, out = pl.pallas_call(
        functools.partial(early_kernel, group, half, early_bases),
        out_shape=[pltpu.VMEM((KVH, GROUP * tokens, 2 * HD), jnp.float32), result],
        in_specs=[vmem_spec] * (2 + len(early)),
        out_specs=[vmem_spec, any_spec],
        scratch_shapes=out_scratch,
        compiler_params=params,
        cost_estimate=pl.CostEstimate(flops=1, bytes_accessed=1, transcendentals=0),
    )(resident(q), resident(starts), *early)

    arrived = []
    for blocks in (far, cross):
        held = []
        for block in blocks:
            block, summed = lax.optimization_barrier((block, summed))
            held += [block, swap(block)]
        arrived.append([resident(a) for a in held])
    middle, high = arrived
    for reads, rows, bases, late in (
        (lambda pair: pair // half % 2 == 1, tokens, high_bases, high),
        (lambda pair: pair == group, tokens // 2, middle_bases, middle),
    ):
        out = pl.pallas_call(
            functools.partial(late_kernel, reads, rows, early_bases, bases),
            out_shape=result,
            in_specs=[vmem_spec] * 3 + [[vmem_spec] * len(a) for a in (early, late)] + [any_spec],
            out_specs=any_spec,
            scratch_shapes=out_scratch,
            input_output_aliases={3 + len(early) + len(late): 0},
            compiler_params=params,
            cost_estimate=pl.CostEstimate(flops=1, bytes_accessed=1, transcendentals=0),
        )(resident(q), resident(starts), resident(summed), early, late, out)
    return out[None]


def solution(mesh):
    placed = (P("dp", "seq", None), P("dp", "seq", None), P("dp", "seq", None), P())
    return jax.shard_map(
        per_device, mesh=mesh, in_specs=placed, out_specs=P("dp", "seq", None), check_vma=False
    )
```

time: 37.8 us -> 35.4 us (0.937)
  the two profiles are of different devices: /device:TPU:17 before, /device:TPU:16 now
where the time goes in v3:
time: 35.4 us; the launch traced here: 35 us
  Pallas kernels  17.5 us (49%)
  waiting for transfers between devices  9.36 us (26%)
  starting transfers between devices  7.23 us (20%)
  other arithmetic  0.6 us (2%)
    pallas_call x2, Pallas kernels, per_device(): pl.pallas_call(functools.partial(late_kernel, reads, rows, early_bases, b...  13 us
    ppermute x5, waiting for transfers between devices, send(): return lax.ppermute(block, 'seq', closed(devices, seq_count))  6.53 us
    ppermute x5, starting transfers between devices, send(): return lax.ppermute(block, 'seq', closed(devices, seq_count))  6.13 us
    ppermute x6, waiting for transfers between devices, swap(): lax.ppermute(block, 'seq', [(2 * c + i, 2 * c + 1 - i) for c in range(pai...  2.83 us
    pallas_call x1, Pallas kernels, per_device(): pl.pallas_call(functools.partial(early_kernel, group, half, early_bases),...  2.19 us
    pallas_call x1, Pallas kernels, per_device(): pl.pallas_call(load_kernel, out_shape=pltpu.VMEM((tokens, QH * HD), jnp.b...  1.23 us
    ppermute x6, starting transfers between devices, swap(): lax.ppermute(block, 'seq', [(2 * c + i, 2 * c + 1 - i) for c in range(pai...  1.09 us
    pallas_call x1, Pallas kernels, per_device(): pl.pallas_call(join_kernel, out_shape=pltpu.VMEM((tokens, 2 * KVH * HD),...  1 us
  transfers between devices with their start and end apart: 11, of which 9 were waited for; matrix products, arithmetic and copies ran while one was open for 2% of the time, Pallas kernels for 10%

profile of v3, /device:TPU:16, one launch (start us, length us, event | category | flops | bytes accessed | tf_op | source)
XLA Modules:
  0.0 35.0 jit_solution(4998180071967410997)
XLA Ops:
  0.0 1.0 %shard_map.46.refs_0_.early_0_ = bf16[64,2048]{1,0:T(8,128)(2,1)S(1)} custom-call(bf16[64,1024]{1,0:T(8,128)(2,1)} %bitcast.11, bf16[64,1024]{1,0:T(8,128)(2,1)} %bitcast.12), custom_call_target="tpu_custom_call" | custom-call | tf_op jit(solution)/shard_map/pallas_call | solution.py:210
  1.1 1.6 %collective-permute-start = (bf16[64,2048]{1,0:T(8,128)(2,1)S(1)}, bf16[64,2048]{1,0:T(8,128)(2,1)S(1)}, u32[]{:S(2)}, u32[]{:S(2)}) collective-permute-start(bf16[64,2048]{1,0:T(8,128)(2,1)S(1)} %shard_map.46.refs_0_.early_0_), channel_id=1, source_target_pairs={{0,4},{1,5},{2,6},{3,7},{4,8},{5,9},{6,2},{7,3},{8,12},{9,13},{10,... | collective-permute-start | bytes 786440 | tf_op jit(solution)/shard_map/ppermute | solution.py:195
  2.7 1.5 %collective-permute-start.6 = (bf16[64,2048]{1,0:T(8,128)(2,1)S(1)}, bf16[64,2048]{1,0:T(8,128)(2,1)S(1)}, u32[]{:S(2)}, u32[]{:S(2)}) collective-permute-start(bf16[64,2048]{1,0:T(8,128)(2,1)S(1)} %shard_map.46.refs_0_.early_0_), channel_id=1, source_target_pairs={{0,2},{1,3},{2,0},{3,1},{4,6},{5,7},{6,8},{7,9},{8,10},{9,11},{10,... | collective-permute-start | bytes 786440 | tf_op jit(solution)/shard_map/ppermute | solution.py:195
  4.2 0.3 reduce-window.9
  4.5 0.1 slice.10
  4.6 1.2 %shard_map.47.q = bf16[64,8192]{1,0:T(8,128)(2,1)S(1)} custom-call(bf16[64,8192]{1,0:T(8,128)(2,1)} %bitcast.10), custom_call_target="tpu_custom_call" | custom-call | tf_op jit(solution)/shard_map/pallas_call | solution.py:237
  5.9 0.1 slice_reduce_fusion
  6.0 3.8 %collective-permute-done.refs_2_.early_2_ = bf16[64,2048]{1,0:T(8,128)(2,1)S(1)} collective-permute-done((bf16[64,2048]{1,0:T(8,128)(2,1)S(1)}, bf16[64,2048]{1,0:T(8,128)(2,1)S(1)}, u32[]{:S(2)}, u32[]{:S(2)}) %collective-permute-start) | collective-permute-done | bytes 262176 | tf_op jit(solution)/shard_map/ppermute | solution.py:195
  9.8 0.4 %collective-permute-start.3 = (bf16[64,2048]{1,0:T(8,128)(2,1)S(1)}, bf16[64,2048]{1,0:T(8,128)(2,1)S(1)}, u32[]{:S(2)}, u32[]{:S(2)}) collective-permute-start(bf16[64,2048]{1,0:T(8,128)(2,1)S(1)} %collective-permute-done.refs_2_.early_2_), channel_id=1, source_target_pairs={{0,1},{1,0},{2,3},{3,2},{4,8},{5,9},{6,7},{7,6},{8,4},{9,5},{10,11... | collective-permute-start | bytes 786440 | tf_op jit(solution)/shard_map/ppermute | solution.py:195
  10.2 1.0 %collective-permute-start.2 = (bf16[64,2048]{1,0:T(8,128)(2,1)S(1)}, bf16[64,2048]{1,0:T(8,128)(2,1)S(1)}, u32[]{:S(2)}, u32[]{:S(2)}) collective-permute-start(bf16[64,2048]{1,0:T(8,128)(2,1)S(1)} %collective-permute-done.refs_2_.early_2_), channel_id=1, source_target_pairs={{0,1},{1,0},{2,3},{3,2},{4,5},{5,4},{6,8},{7,9},{8,10},{9,11},{10,... | collective-permute-start | bytes 786440 | tf_op jit(solution)/shard_map/ppermute | solution.py:195
  11.3 1.5 %collective-permute-start.1 = (bf16[64,2048]{1,0:T(8,128)(2,1)S(1)}, bf16[64,2048]{1,0:T(8,128)(2,1)S(1)}, u32[]{:S(2)}, u32[]{:S(2)}) collective-permute-start(bf16[64,2048]{1,0:T(8,128)(2,1)S(1)} %shard_map.46.refs_0_.early_0_), channel_id=1, source_target_pairs={{0,6},{1,7},{2,4},{3,5},{4,0},{5,1},{6,2},{7,3},{8,14},{9,15},{10,... | collective-permute-start | bytes 786440 | tf_op jit(solution)/shard_map/ppermute | solution.py:195
  12.8 0.5 %collective-permute-start.7 = (bf16[64,2048]{1,0:T(8,128)(2,1)S(1)}, bf16[64,2048]{1,0:T(8,128)(2,1)S(1)}, u32[]{:S(2)}, u32[]{:S(2)}) collective-permute-start(bf16[64,2048]{1,0:T(8,128)(2,1)S(1)} %collective-permute-done.6.refs_4_.early_4_), channel_id=1, source_target_pairs={{0,1},{1,0},{2,3},{3,2},{4,5},{5,4},{6,7},{7,6},{8,9},{9,8},{10,11... | collective-permute-start | bytes 786440 | tf_op jit(solution)/shard_map/ppermute | solution.py:198
  13.4 0.2 select_reduce_fusion
  13.6 0.8 %collective-permute-done.5.refs_3_.early_3_ = bf16[64,2048]{1,0:T(8,128)(2,1)S(1)} collective-permute-done((bf16[64,2048]{1,0:T(8,128)(2,1)S(1)}, bf16[64,2048]{1,0:T(8,128)(2,1)S(1)}, u32[]{:S(2)}, u32[]{:S(2)}) %collective-permute-start.5) | collective-permute-done | bytes 262176 | tf_op jit(solution)/shard_map/ppermute | solution.py:198
  14.3 0.4 %collective-permute-done.7.refs_5_.early_5_ = bf16[64,2048]{1,0:T(8,128)(2,1)S(1)} collective-permute-done((bf16[64,2048]{1,0:T(8,128)(2,1)S(1)}, bf16[64,2048]{1,0:T(8,128)(2,1)S(1)}, u32[]{:S(2)}, u32[]{:S(2)}) %collective-permute-start.7) | collective-permute-done | bytes 262176 | tf_op jit(solution)/shard_map/ppermute | solution.py:198
  14.8 2.2 %shard_map.48 = (f32[8,512,256]{2,1,0:T(8,128)S(1)}, bf16[64,8192]{1,0:T(8,128)(2,1)}) custom-call(bf16[64,8192]{1,0:T(8,128)(2,1)S(1)} %shard_map.47.q, s32[64,128]{1,0:T(8,128)S(1)} %broadcast_in_dim.18.starts, bf16[64,2048]{1,0:T(8,128)(2,1)S(1)} %shard_map.46.refs_0_.early_0_, bf16[64,2048]{1,0:T(8,128)(2,1)S(1)} %collective-permute-done.4.refs_1_.early_1_, ...), custom_call_target="tpu_custom_call" | custom-call | flops 1 | bytes 1 | tf_op jit(solution)/shard_map/pallas_call | solution.py:310
  17.0 0.7 %collective-permute-done.3.late_0_ = bf16[64,2048]{1,0:T(8,128)(2,1)S(1)} collective-permute-done((bf16[64,2048]{1,0:T(8,128)(2,1)S(1)}, bf16[64,2048]{1,0:T(8,128)(2,1)S(1)}, u32[]{:S(2)}, u32[]{:S(2)}) %collective-permute-start.3) | collective-permute-done | bytes 262176 | tf_op jit(solution)/shard_map/ppermute | solution.py:195
  17.7 1.1 %collective-permute-done.2.late_2_ = bf16[64,2048]{1,0:T(8,128)(2,1)S(1)} collective-permute-done((bf16[64,2048]{1,0:T(8,128)(2,1)S(1)}, bf16[64,2048]{1,0:T(8,128)(2,1)S(1)}, u32[]{:S(2)}, u32[]{:S(2)}) %collective-permute-start.2) | collective-permute-done | bytes 262176 | tf_op jit(solution)/shard_map/ppermute | solution.py:195
  18.7 1.0 %collective-permute-done.1.late_0_ = bf16[64,2048]{1,0:T(8,128)(2,1)S(1)} collective-permute-done((bf16[64,2048]{1,0:T(8,128)(2,1)S(1)}, bf16[64,2048]{1,0:T(8,128)(2,1)S(1)}, u32[]{:S(2)}, u32[]{:S(2)}) %collective-permute-start.1) | collective-permute-done | bytes 262176 | tf_op jit(solution)/shard_map/ppermute | solution.py:195
  19.7 0.5 %collective-permute-start.9 = (bf16[64,2048]{1,0:T(8,128)(2,1)S(1)}, bf16[64,2048]{1,0:T(8,128)(2,1)S(1)}, u32[]{:S(2)}, u32[]{:S(2)}) collective-permute-start(bf16[64,2048]{1,0:T(8,128)(2,1)S(1)} %collective-permute-done.2.late_2_), channel_id=1, source_target_pairs={{0,1},{1,0},{2,3},{3,2},{4,5},{5,4},{6,7},{7,6},{8,9},{9,8},{10,11... | collective-permute-start | bytes 786440 | tf_op jit(solution)/shard_map/ppermute | solution.py:198
  20.2 1.0 %collective-permute-done.10.late_1_ = bf16[64,2048]{1,0:T(8,128)(2,1)S(1)} collective-permute-done((bf16[64,2048]{1,0:T(8,128)(2,1)S(1)}, bf16[64,2048]{1,0:T(8,128)(2,1)S(1)}, u32[]{:S(2)}, u32[]{:S(2)}) %collective-permute-start.10) | collective-permute-done | bytes 262176 | tf_op jit(solution)/shard_map/ppermute | solution.py:198
  21.3 0.3 collective-permute-done.9.late_3_
  21.6 0.4 %collective-permute-done.8.late_1_ = bf16[64,2048]{1,0:T(8,128)(2,1)S(1)} collective-permute-done((bf16[64,2048]{1,0:T(8,128)(2,1)S(1)}, bf16[64,2048]{1,0:T(8,128)(2,1)S(1)}, u32[]{:S(2)}, u32[]{:S(2)}) %collective-permute-start.8) | collective-permute-done | bytes 262176 | tf_op jit(solution)/shard_map/ppermute | solution.py:198
  22.0 13.0 %shard_map.50 = bf16[64,8192]{1,0:T(8,128)(2,1)} custom-call(bf16[64,8192]{1,0:T(8,128)(2,1)S(1)} %shard_map.47.q, s32[64,128]{1,0:T(8,128)S(1)} %broadcast_in_dim.18.starts, f32[8,512,256]{2,1,0:T(8,128)S(1)} %get-tuple-element.24.summed, bf16[64,2048]{1,0:T(8,128)(2,1)S(1)} %shard_map.46.refs_0_.early_0_, ...), custom_call_target="tpu_custom_call", output_to_operand_aliasing={{}: (13, {})} | custom-call | flops 1 | bytes 1 | tf_op jit(solution)/shard_map/pallas_call | solution.py:332
  (15 shorter events, 0.4 us)
Async XLA Ops:
  0.0 4.2 %copy-start = (s32[2,129]{1,0:T(2,128)S(1)}, s32[2,129]{1,0:T(2,128)}, u32[]{:S(2)}) copy-start(s32[2,129]{1,0:T(2,128)} %param.7) | copy-start | bytes 3100
  1.0 1.7 %collective-permute-start.4 = (bf16[64,2048]{1,0:T(8,128)(2,1)S(1)}, bf16[64,2048]{1,0:T(8,128)(2,1)S(1)}, u32[]{:S(2)}, u32[]{:S(2)}) collective-permute-start(bf16[64,2048]{1,0:T(8,128)(2,1)S(1)} %shard_map.46.refs_0_.early_0_), channel_id=1, source_target_pairs={{0,1},{1,0},{2,3},{3,2},{4,5},{5,4},{6,7},{7,6},{8,9},{9,8},{10,11... | collective-permute-start | bytes 786440 | tf_op jit(solution)/shard_map/ppermute | solution.py:198
  1.1 8.7 %collective-permute-start = (bf16[64,2048]{1,0:T(8,128)(2,1)S(1)}, bf16[64,2048]{1,0:T(8,128)(2,1)S(1)}, u32[]{:S(2)}, u32[]{:S(2)}) collective-permute-start(bf16[64,2048]{1,0:T(8,128)(2,1)S(1)} %shard_map.46.refs_0_.early_0_), channel_id=1, source_target_pairs={{0,4},{1,5},{2,6},{3,7},{4,8},{5,9},{6,2},{7,3},{8,12},{9,13},{10,... | collective-permute-start | bytes 786440 | tf_op jit(solution)/shard_map/ppermute | solution.py:195
  2.7 10.1 %collective-permute-start.6 = (bf16[64,2048]{1,0:T(8,128)(2,1)S(1)}, bf16[64,2048]{1,0:T(8,128)(2,1)S(1)}, u32[]{:S(2)}, u32[]{:S(2)}) collective-permute-start(bf16[64,2048]{1,0:T(8,128)(2,1)S(1)} %shard_map.46.refs_0_.early_0_), channel_id=1, source_target_pairs={{0,2},{1,3},{2,0},{3,1},{4,6},{5,7},{6,8},{7,9},{8,10},{9,11},{10,... | collective-permute-start | bytes 786440 | tf_op jit(solution)/shard_map/ppermute | solution.py:195
  9.8 7.9 %collective-permute-start.3 = (bf16[64,2048]{1,0:T(8,128)(2,1)S(1)}, bf16[64,2048]{1,0:T(8,128)(2,1)S(1)}, u32[]{:S(2)}, u32[]{:S(2)}) collective-permute-start(bf16[64,2048]{1,0:T(8,128)(2,1)S(1)} %collective-permute-done.refs_2_.early_2_), channel_id=1, source_target_pairs={{0,1},{1,0},{2,3},{3,2},{4,8},{5,9},{6,7},{7,6},{8,4},{9,5},{10,11... | collective-permute-start | bytes 786440 | tf_op jit(solution)/shard_map/ppermute | solution.py:195
  10.2 8.5 %collective-permute-start.2 = (bf16[64,2048]{1,0:T(8,128)(2,1)S(1)}, bf16[64,2048]{1,0:T(8,128)(2,1)S(1)}, u32[]{:S(2)}, u32[]{:S(2)}) collective-permute-start(bf16[64,2048]{1,0:T(8,128)(2,1)S(1)} %collective-permute-done.refs_2_.early_2_), channel_id=1, source_target_pairs={{0,1},{1,0},{2,3},{3,2},{4,5},{5,4},{6,8},{7,9},{8,10},{9,11},{10,... | collective-permute-start | bytes 786440 | tf_op jit(solution)/shard_map/ppermute | solution.py:195
  11.3 8.4 %collective-permute-start.1 = (bf16[64,2048]{1,0:T(8,128)(2,1)S(1)}, bf16[64,2048]{1,0:T(8,128)(2,1)S(1)}, u32[]{:S(2)}, u32[]{:S(2)}) collective-permute-start(bf16[64,2048]{1,0:T(8,128)(2,1)S(1)} %shard_map.46.refs_0_.early_0_), channel_id=1, source_target_pairs={{0,6},{1,7},{2,4},{3,5},{4,0},{5,1},{6,2},{7,3},{8,14},{9,15},{10,... | collective-permute-start | bytes 786440 | tf_op jit(solution)/shard_map/ppermute | solution.py:195
  12.8 1.5 %collective-permute-start.5 = (bf16[64,2048]{1,0:T(8,128)(2,1)S(1)}, bf16[64,2048]{1,0:T(8,128)(2,1)S(1)}, u32[]{:S(2)}, u32[]{:S(2)}) collective-permute-start(bf16[64,2048]{1,0:T(8,128)(2,1)S(1)} %collective-permute-done.refs_2_.early_2_), channel_id=1, source_target_pairs={{0,1},{1,0},{2,3},{3,2},{4,5},{5,4},{6,7},{7,6},{8,9},{9,8},{10,11... | collective-permute-start | bytes 786440 | tf_op jit(solution)/shard_map/ppermute | solution.py:198
  12.8 1.9 %collective-permute-start.7 = (bf16[64,2048]{1,0:T(8,128)(2,1)S(1)}, bf16[64,2048]{1,0:T(8,128)(2,1)S(1)}, u32[]{:S(2)}, u32[]{:S(2)}) collective-permute-start(bf16[64,2048]{1,0:T(8,128)(2,1)S(1)} %collective-permute-done.6.refs_4_.early_4_), channel_id=1, source_target_pairs={{0,1},{1,0},{2,3},{3,2},{4,5},{5,4},{6,7},{7,6},{8,9},{9,8},{10,11... | collective-permute-start | bytes 786440 | tf_op jit(solution)/shard_map/ppermute | solution.py:198
  19.7 1.5 %collective-permute-start.10 = (bf16[64,2048]{1,0:T(8,128)(2,1)S(1)}, bf16[64,2048]{1,0:T(8,128)(2,1)S(1)}, u32[]{:S(2)}, u32[]{:S(2)}) collective-permute-start(bf16[64,2048]{1,0:T(8,128)(2,1)S(1)} %collective-permute-done.1.late_0_), channel_id=1, source_target_pairs={{0,1},{1,0},{2,3},{3,2},{4,5},{5,4},{6,7},{7,6},{8,9},{9,8},{10,11... | collective-permute-start | bytes 786440 | tf_op jit(solution)/shard_map/ppermute | solution.py:198
  19.7 1.9 %collective-permute-start.9 = (bf16[64,2048]{1,0:T(8,128)(2,1)S(1)}, bf16[64,2048]{1,0:T(8,128)(2,1)S(1)}, u32[]{:S(2)}, u32[]{:S(2)}) collective-permute-start(bf16[64,2048]{1,0:T(8,128)(2,1)S(1)} %collective-permute-done.2.late_2_), channel_id=1, source_target_pairs={{0,1},{1,0},{2,3},{3,2},{4,5},{5,4},{6,7},{7,6},{8,9},{9,8},{10,11... | collective-permute-start | bytes 786440 | tf_op jit(solution)/shard_map/ppermute | solution.py:198
  20.2 1.8 %collective-permute-start.8 = (bf16[64,2048]{1,0:T(8,128)(2,1)S(1)}, bf16[64,2048]{1,0:T(8,128)(2,1)S(1)}, u32[]{:S(2)}, u32[]{:S(2)}) collective-permute-start(bf16[64,2048]{1,0:T(8,128)(2,1)S(1)} %collective-permute-done.3.late_0_), channel_id=1, source_target_pairs={{0,1},{1,0},{2,3},{3,2},{4,5},{5,4},{6,7},{7,6},{8,9},{9,8},{10,11... | collective-permute-start | bytes 786440 | tf_op jit(solution)/shard_map/ppermute | solution.py:198

commit v4 on v3

--- a/solution.py
+++ b/solution.py
@@ -243,32 +243,30 @@
         compiler_params=params,
     )(in_hbm(queries[0]))
     first[0], q = lax.optimization_barrier((first[0], q))
+    is_high = lax.axis_index("seq") // 2 // half % 2 == 1
+    mixed = jnp.where(is_high, first[0], own)
+
+    def across(step):
+        return [(lo + (j - step) % half, lo + half + j) for lo in (0, group) for j in range(half)]
+
+    back = [(half + j, j) for j in range(half) if j != 1]
+    back += [(group + half + j, group + j) for j in range(2, half)]
+    back += [(group + half, group + 1), (group + half + 1, 1)]
+    merged = across(1) + [(half + 1, group)] + back
+    both = [send(mixed, [(a, c, b, c) for a, b in merged for c in (0, 1)])]
     own_later, _ = lax.optimization_barrier((own, first[0]))
-    came_up = first[0]
-    cross = [
-        send(
-            own_later,
-            [
-                (lo + (j - step) % half, core, lo + half + j, core)
-                for lo in (0, group)
-                for j in range(half)
-                for core in (0, 1)
-            ]
-            + [
-                (lo + half + j, core, lo + j, core)
-                for lo in (0, group)
-                for j in range(half)
-                for core in (0, 1)
-            ],
-        )
-        for step in range(1, half)
+    cross = both + [
+        send(own_later, [(a, c, b, c) for a, b in across(step) for c in (0, 1)])
+        for step in range(2, half)
     ]
     far = []
     for j in range(half):
-        back = [] if j % 2 == 0 else [group + 1]
-        route = [half + j, group, *back, half + j]
+        if j == 1:
+            far += both
+            continue
+        path = [half + j, group, *([group + 1] if j % 2 else []), half + j]
         far.append(
-            send(came_up, [(a, c, b, c) for a, b in zip(route, route[1:]) for c in (0, 1)])
+            send(first[0], [(a, c, b, c) for a, b in zip(path, path[1:]) for c in (0, 1)])
         )
 
     def position(source, core, tokens, valid):
@@ -317,13 +315,15 @@
         cost_estimate=pl.CostEstimate(flops=1, bytes_accessed=1, transcendentals=0),
     )(resident(q), resident(starts), *early)
 
-    arrived = []
+    seen, arrived = {}, []
     for blocks in (far, cross):
         held = []
         for block in blocks:
-            block, summed = lax.optimization_barrier((block, summed))
-            held += [block, swap(block)]
-        arrived.append([resident(a) for a in held])
+            if id(block) not in seen:
+                tied, summed = lax.optimization_barrier((block, summed))
+                seen[id(block)] = [resident(tied), resident(swap(tied))]
+            held += seen[id(block)]
+        arrived.append(held)
     middle, high = arrived
     for reads, rows, bases, late in (
         (lambda pair: pair // half % 2 == 1, tokens, high_bases, high),

time: 35.4 us -> 34.8 us (0.983)
  starting transfers between devices: 7.23 us -> 6.54 us
    ppermute x5 -> x4, starting transfers between devices: 6.13 us -> 5.73 us  [send(): return lax.ppermute(block, 'seq', closed(devices, seq_count))]
    ppermute x6 -> x5, starting transfers between devices: 1.09 us -> 0.81 us  [swap(): lax.ppermute(block, 'seq', [(2 * c + i, 2 * c + 1 - i) for c in range(pai...]
    ppermute x5 -> x4, waiting for transfers between devices: 6.53 us -> 6.77 us  [send(): return lax.ppermute(block, 'seq', closed(devices, seq_count))]
    ppermute x6 -> x5, waiting for transfers between devices: 2.83 us -> 2.59 us  [swap(): lax.ppermute(block, 'seq', [(2 * c + i, 2 * c + 1 - i) for c in range(pai...]
  transfers between devices with their start and end apart: 11 -> 9, of which waited for: 9 -> 6; matrix products, arithmetic and copies ran while one was open for 2% -> 3% of each run, Pallas kernels for 10% -> 10%
where the time goes in v4:
time: 34.8 us; the launch traced here: 34.3 us
  Pallas kernels  17.5 us (50%)
  waiting for transfers between devices  9.36 us (27%)
  starting transfers between devices  6.54 us (19%)
  other arithmetic  0.63 us (2%)
    pallas_call x2, Pallas kernels, per_device(): pl.pallas_call(functools.partial(late_kernel, reads, rows, early_bases, b...  13 us
    ppermute x4, waiting for transfers between devices, send(): return lax.ppermute(block, 'seq', closed(devices, seq_count))  6.77 us
    ppermute x4, starting transfers between devices, send(): return lax.ppermute(block, 'seq', closed(devices, seq_count))  5.73 us
    ppermute x5, waiting for transfers between devices, swap(): lax.ppermute(block, 'seq', [(2 * c + i, 2 * c + 1 - i) for c in range(pai...  2.59 us
    pallas_call x1, Pallas kernels, per_device(): pl.pallas_call(functools.partial(early_kernel, group, half, early_bases),...  2.19 us
    pallas_call x1, Pallas kernels, per_device(): pl.pallas_call(load_kernel, out_shape=pltpu.VMEM((tokens, QH * HD), jnp.b...  1.23 us
    pallas_call x1, Pallas kernels, per_device(): pl.pallas_call(join_kernel, out_shape=pltpu.VMEM((tokens, 2 * KVH * HD),...  1 us
    ppermute x5, starting transfers between devices, swap(): lax.ppermute(block, 'seq', [(2 * c + i, 2 * c + 1 - i) for c in range(pai...  0.81 us
  transfers between devices with their start and end apart: 9, of which 6 were waited for; matrix products, arithmetic and copies ran while one was open for 3% of the time, Pallas kernels for 10%

profile of v4, /device:TPU:16, one launch (start us, length us, event | category | flops | bytes accessed | tf_op | source)
XLA Modules:
  0.0 34.3 jit_solution(8031277370494504977)
XLA Ops:
  0.0 1.0 %shard_map.46.refs_0_.early_0_ = bf16[64,2048]{1,0:T(8,128)(2,1)S(1)} custom-call(bf16[64,1024]{1,0:T(8,128)(2,1)} %bitcast.11, bf16[64,1024]{1,0:T(8,128)(2,1)} %bitcast.12), custom_call_target="tpu_custom_call" | custom-call | tf_op jit(solution)/shard_map/pallas_call | solution.py:210
  1.0 0.1 collective-permute-start.3
  1.1 1.6 %collective-permute-start = (bf16[64,2048]{1,0:T(8,128)(2,1)S(1)}, bf16[64,2048]{1,0:T(8,128)(2,1)S(1)}, u32[]{:S(2)}, u32[]{:S(2)}) collective-permute-start(bf16[64,2048]{1,0:T(8,128)(2,1)S(1)} %shard_map.46.refs_0_.early_0_), channel_id=1, source_target_pairs={{0,4},{1,5},{2,6},{3,7},{4,8},{5,9},{6,2},{7,3},{8,12},{9,13},{10,... | collective-permute-start | bytes 786440 | tf_op jit(solution)/shard_map/ppermute | solution.py:195
  2.7 0.3 reduce-window.9
  3.0 0.1 slice.10
  3.2 1.2 %shard_map.47.q = bf16[64,8192]{1,0:T(8,128)(2,1)S(1)} custom-call(bf16[64,8192]{1,0:T(8,128)(2,1)} %bitcast.10), custom_call_target="tpu_custom_call" | custom-call | tf_op jit(solution)/shard_map/pallas_call | solution.py:237
  4.4 0.1 slice_reduce_fusion
  4.5 1.5 %collective-permute-start.5 = (bf16[64,2048]{1,0:T(8,128)(2,1)S(1)}, bf16[64,2048]{1,0:T(8,128)(2,1)S(1)}, u32[]{:S(2)}, u32[]{:S(2)}) collective-permute-start(bf16[64,2048]{1,0:T(8,128)(2,1)S(1)} %shard_map.46.refs_0_.early_0_), channel_id=1, source_target_pairs={{0,2},{1,3},{2,0},{3,1},{4,6},{5,7},{6,8},{7,9},{8,10},{9,11},{10,... | collective-permute-start | bytes 786440 | tf_op jit(solution)/shard_map/ppermute | solution.py:195
  6.1 3.7 %collective-permute-done.refs_2_.early_2_ = bf16[64,2048]{1,0:T(8,128)(2,1)S(1)} collective-permute-done((bf16[64,2048]{1,0:T(8,128)(2,1)S(1)}, bf16[64,2048]{1,0:T(8,128)(2,1)S(1)}, u32[]{:S(2)}, u32[]{:S(2)}) %collective-permute-start) | collective-permute-done | bytes 262176 | tf_op jit(solution)/shard_map/ppermute | solution.py:195
  9.8 0.4 %collective-permute-start.2 = (bf16[64,2048]{1,0:T(8,128)(2,1)S(1)}, bf16[64,2048]{1,0:T(8,128)(2,1)S(1)}, u32[]{:S(2)}, u32[]{:S(2)}) collective-permute-start(bf16[64,2048]{1,0:T(8,128)(2,1)S(1)} %collective-permute-done.refs_2_.early_2_), channel_id=1, source_target_pairs={{0,1},{1,0},{2,3},{3,2},{4,8},{5,9},{6,7},{7,6},{8,4},{9,5},{10,11... | collective-permute-start | bytes 786440 | tf_op jit(solution)/shard_map/ppermute | solution.py:195
  10.3 2.1 %collective-permute-start.1 = (bf16[64,2048]{1,0:T(8,128)(2,1)S(1)}, bf16[64,2048]{1,0:T(8,128)(2,1)S(1)}, u32[]{:S(2)}, u32[]{:S(2)}) collective-permute-start(bf16[64,2048]{1,0:T(8,128)(2,1)S(1)} %broadcast_select_fusion), channel_id=1, source_target_pairs={{0,6},{1,7},{2,4},{3,5},{4,0},{5,1},{6,8},{7,9},{8,14},{9,15},{10,... | collective-permute-start | bytes 786440 | tf_op jit(solution)/shard_map/ppermute | solution.py:195
  12.4 0.2 collective-permute-start.4
  12.6 1.8 %collective-permute-done.5.refs_4_.early_4_ = bf16[64,2048]{1,0:T(8,128)(2,1)S(1)} collective-permute-done((bf16[64,2048]{1,0:T(8,128)(2,1)S(1)}, bf16[64,2048]{1,0:T(8,128)(2,1)S(1)}, u32[]{:S(2)}, u32[]{:S(2)}) %collective-permute-start.5) | collective-permute-done | bytes 262176 | tf_op jit(solution)/shard_map/ppermute | solution.py:195
  14.4 0.1 add_bitcast_fusion
  14.5 0.2 select_reduce_fusion
  14.7 1.3 %collective-permute-done.6.refs_5_.early_5_ = bf16[64,2048]{1,0:T(8,128)(2,1)S(1)} collective-permute-done((bf16[64,2048]{1,0:T(8,128)(2,1)S(1)}, bf16[64,2048]{1,0:T(8,128)(2,1)S(1)}, u32[]{:S(2)}, u32[]{:S(2)}) %collective-permute-start.6) | collective-permute-done | bytes 262176 | tf_op jit(solution)/shard_map/ppermute | solution.py:198
  15.9 0.1 broadcast_in_dim.18.starts
  16.0 2.2 %shard_map.48 = (f32[8,512,256]{2,1,0:T(8,128)S(1)}, bf16[64,8192]{1,0:T(8,128)(2,1)}) custom-call(bf16[64,8192]{1,0:T(8,128)(2,1)S(1)} %shard_map.47.q, s32[64,128]{1,0:T(8,128)S(1)} %broadcast_in_dim.18.starts, bf16[64,2048]{1,0:T(8,128)(2,1)S(1)} %shard_map.46.refs_0_.early_0_, bf16[64,2048]{1,0:T(8,128)(2,1)S(1)} %collective-permute-done.3.refs_1_.early_1_, ...), custom_call_target="tpu_custom_call" | custom-call | flops 1 | bytes 1 | tf_op jit(solution)/shard_map/pallas_call | solution.py:308
  18.2 1.2 %collective-permute-done.1.late_0_.late_2_ = bf16[64,2048]{1,0:T(8,128)(2,1)S(1)} collective-permute-done((bf16[64,2048]{1,0:T(8,128)(2,1)S(1)}, bf16[64,2048]{1,0:T(8,128)(2,1)S(1)}, u32[]{:S(2)}, u32[]{:S(2)}) %collective-permute-start.1) | collective-permute-done | bytes 262176 | tf_op jit(solution)/shard_map/ppermute | solution.py:195
  19.5 0.5 %collective-permute-start.7 = (bf16[64,2048]{1,0:T(8,128)(2,1)S(1)}, bf16[64,2048]{1,0:T(8,128)(2,1)S(1)}, u32[]{:S(2)}, u32[]{:S(2)}) collective-permute-start(bf16[64,2048]{1,0:T(8,128)(2,1)S(1)} %collective-permute-done.2.late_0_), channel_id=1, source_target_pairs={{0,1},{1,0},{2,3},{3,2},{4,5},{5,4},{6,7},{7,6},{8,9},{9,8},{10,11... | collective-permute-start | bytes 786440 | tf_op jit(solution)/shard_map/ppermute | solution.py:198
  20.0 1.0 %collective-permute-done.8.late_1_.late_3_ = bf16[64,2048]{1,0:T(8,128)(2,1)S(1)} collective-permute-done((bf16[64,2048]{1,0:T(8,128)(2,1)S(1)}, bf16[64,2048]{1,0:T(8,128)(2,1)S(1)}, u32[]{:S(2)}, u32[]{:S(2)}) %collective-permute-start.8) | collective-permute-done | bytes 262176 | tf_op jit(solution)/shard_map/ppermute | solution.py:198
  21.0 0.1 shard_map.49._
  21.1 0.3 collective-permute-done.7.late_1_
  21.4 13.0 %shard_map.50 = bf16[64,8192]{1,0:T(8,128)(2,1)} custom-call(bf16[64,8192]{1,0:T(8,128)(2,1)S(1)} %shard_map.47.q, s32[64,128]{1,0:T(8,128)S(1)} %broadcast_in_dim.18.starts, f32[8,512,256]{2,1,0:T(8,128)S(1)} %get-tuple-element.19.summed, bf16[64,2048]{1,0:T(8,128)(2,1)S(1)} %shard_map.46.refs_0_.early_0_, ...), custom_call_target="tpu_custom_call", output_to_operand_aliasing={{}: (13, {})} | custom-call | flops 1 | bytes 1 | tf_op jit(solution)/shard_map/pallas_call | solution.py:332
  (12 shorter events, 0.1 us)
Async XLA Ops:
  0.0 2.7 %copy-start = (s32[2,129]{1,0:T(2,128)S(1)}, s32[2,129]{1,0:T(2,128)}, u32[]{:S(2)}) copy-start(s32[2,129]{1,0:T(2,128)} %param.7) | copy-start | bytes 3100
  1.0 3.5 %collective-permute-start.3 = (bf16[64,2048]{1,0:T(8,128)(2,1)S(1)}, bf16[64,2048]{1,0:T(8,128)(2,1)S(1)}, u32[]{:S(2)}, u32[]{:S(2)}) collective-permute-start(bf16[64,2048]{1,0:T(8,128)(2,1)S(1)} %shard_map.46.refs_0_.early_0_), channel_id=1, source_target_pairs={{0,1},{1,0},{2,3},{3,2},{4,5},{5,4},{6,7},{7,6},{8,9},{9,8},{10,11... | collective-permute-start | bytes 786440 | tf_op jit(solution)/shard_map/ppermute | solution.py:198
  1.1 8.7 %collective-permute-start = (bf16[64,2048]{1,0:T(8,128)(2,1)S(1)}, bf16[64,2048]{1,0:T(8,128)(2,1)S(1)}, u32[]{:S(2)}, u32[]{:S(2)}) collective-permute-start(bf16[64,2048]{1,0:T(8,128)(2,1)S(1)} %shard_map.46.refs_0_.early_0_), channel_id=1, source_target_pairs={{0,4},{1,5},{2,6},{3,7},{4,8},{5,9},{6,2},{7,3},{8,12},{9,13},{10,... | collective-permute-start | bytes 786440 | tf_op jit(solution)/shard_map/ppermute | solution.py:195
  4.5 9.9 %collective-permute-start.5 = (bf16[64,2048]{1,0:T(8,128)(2,1)S(1)}, bf16[64,2048]{1,0:T(8,128)(2,1)S(1)}, u32[]{:S(2)}, u32[]{:S(2)}) collective-permute-start(bf16[64,2048]{1,0:T(8,128)(2,1)S(1)} %shard_map.46.refs_0_.early_0_), channel_id=1, source_target_pairs={{0,2},{1,3},{2,0},{3,1},{4,6},{5,7},{6,8},{7,9},{8,10},{9,11},{10,... | collective-permute-start | bytes 786440 | tf_op jit(solution)/shard_map/ppermute | solution.py:195
  9.8 8.4 %collective-permute-start.2 = (bf16[64,2048]{1,0:T(8,128)(2,1)S(1)}, bf16[64,2048]{1,0:T(8,128)(2,1)S(1)}, u32[]{:S(2)}, u32[]{:S(2)}) collective-permute-start(bf16[64,2048]{1,0:T(8,128)(2,1)S(1)} %collective-permute-done.refs_2_.early_2_), channel_id=1, source_target_pairs={{0,1},{1,0},{2,3},{3,2},{4,8},{5,9},{6,7},{7,6},{8,4},{9,5},{10,11... | collective-permute-start | bytes 786440 | tf_op jit(solution)/shard_map/ppermute | solution.py:195
  10.3 9.2 %collective-permute-start.1 = (bf16[64,2048]{1,0:T(8,128)(2,1)S(1)}, bf16[64,2048]{1,0:T(8,128)(2,1)S(1)}, u32[]{:S(2)}, u32[]{:S(2)}) collective-permute-start(bf16[64,2048]{1,0:T(8,128)(2,1)S(1)} %broadcast_select_fusion), channel_id=1, source_target_pairs={{0,6},{1,7},{2,4},{3,5},{4,0},{5,1},{6,8},{7,9},{8,14},{9,15},{10,... | collective-permute-start | bytes 786440 | tf_op jit(solution)/shard_map/ppermute | solution.py:195
  12.4 2.3 %collective-permute-start.4 = (bf16[64,2048]{1,0:T(8,128)(2,1)S(1)}, bf16[64,2048]{1,0:T(8,128)(2,1)S(1)}, u32[]{:S(2)}, u32[]{:S(2)}) collective-permute-start(bf16[64,2048]{1,0:T(8,128)(2,1)S(1)} %collective-permute-done.refs_2_.early_2_), channel_id=1, source_target_pairs={{0,1},{1,0},{2,3},{3,2},{4,5},{5,4},{6,7},{7,6},{8,9},{9,8},{10,11... | collective-permute-start | bytes 786440 | tf_op jit(solution)/shard_map/ppermute | solution.py:198
  14.4 1.5 %collective-permute-start.6 = (bf16[64,2048]{1,0:T(8,128)(2,1)S(1)}, bf16[64,2048]{1,0:T(8,128)(2,1)S(1)}, u32[]{:S(2)}, u32[]{:S(2)}) collective-permute-start(bf16[64,2048]{1,0:T(8,128)(2,1)S(1)} %collective-permute-done.5.refs_4_.early_4_), channel_id=1, source_target_pairs={{0,1},{1,0},{2,3},{3,2},{4,5},{5,4},{6,7},{7,6},{8,9},{9,8},{10,11... | collective-permute-start | bytes 786440 | tf_op jit(solution)/shard_map/ppermute | solution.py:198
  19.5 1.5 %collective-permute-start.8 = (bf16[64,2048]{1,0:T(8,128)(2,1)S(1)}, bf16[64,2048]{1,0:T(8,128)(2,1)S(1)}, u32[]{:S(2)}, u32[]{:S(2)}) collective-permute-start(bf16[64,2048]{1,0:T(8,128)(2,1)S(1)} %collective-permute-done.1.late_0_.late_2_), channel_id=1, source_target_pairs={{0,1},{1,0},{2,3},{3,2},{4,5},{5,4},{6,7},{7,6},{8,9},{9,8},{10,11... | collective-permute-start | bytes 786440 | tf_op jit(solution)/shard_map/ppermute | solution.py:198
  19.5 1.9 %collective-permute-start.7 = (bf16[64,2048]{1,0:T(8,128)(2,1)S(1)}, bf16[64,2048]{1,0:T(8,128)(2,1)S(1)}, u32[]{:S(2)}, u32[]{:S(2)}) collective-permute-start(bf16[64,2048]{1,0:T(8,128)(2,1)S(1)} %collective-permute-done.2.late_0_), channel_id=1, source_target_pairs={{0,1},{1,0},{2,3},{3,2},{4,5},{5,4},{6,7},{7,6},{8,9},{9,8},{10,11... | collective-permute-start | bytes 786440 | tf_op jit(solution)/shard_map/ppermute | solution.py:198

commit v5 on v4

--- a/solution.py
+++ b/solution.py
@@ -16,6 +16,7 @@
 MASKED = -1e30
 EXPONENT_SCALE = math.log2(math.e) / math.sqrt(HD)
 LOW_TOTAL, HIGH_TOTAL = 2.0**-60, 2.0**80
+MARK_BYTES = 64 * 1024 * 1024
 VMEM_LIMIT = 24 * 1024 * 1024
 
 
@@ -70,6 +71,10 @@
     return jnp.dot(weights, v, preferred_element_type=jnp.float32)
 
 
+def mark_kernel(block, mark):
+    mark[...] = block[:16, :HD]
+
+
 def load_kernel(source, target, sem):
     copy = pltpu.make_async_copy(source, target, sem)
     copy.start()
@@ -90,16 +95,15 @@
 
 def finish(totals_of, spans, q, starts, first_position, out, out_hbm, sems):
     tokens = q.shape[0]
-    faults = jnp.zeros((GROUP * tokens, HD), jnp.float32)
+    lowest = highest = jnp.ones((GROUP * tokens, HD), jnp.float32)
     for g in range(KVH):
         totals = totals_of(g)
         for (first, *_), total in zip(spans, totals):
             store(g, first, total, out)
         weights = jnp.concatenate([total[:, HD:] for total in totals], axis=0)
-        sound = (weights > LOW_TOTAL) & (weights < HIGH_TOTAL)
-        faults = jnp.maximum(faults, jnp.where(sound, 0.0, 1.0))
+        lowest, highest = jnp.minimum(lowest, weights), jnp.maximum(highest, weights)
         copy_out(g, out, out_hbm, sems).start()
-    any_fault = jnp.max(faults) > 0.0
+    any_fault = jnp.max(jnp.maximum(LOW_TOTAL / lowest, highest / HIGH_TOTAL)) >= 1.0
     for g in range(KVH):
         copy_out(g, out, out_hbm, sems).wait()
 
@@ -234,6 +238,7 @@
         for d in distances
     ]
     swapped = [swap(block) for block in first]
+    waiting, _ = lax.optimization_barrier((queries[0], sibling))
     q = pl.pallas_call(
         load_kernel,
         out_shape=pltpu.VMEM((tokens, QH * HD), jnp.bfloat16),
@@ -241,10 +246,19 @@
         out_specs=vmem_spec,
         scratch_shapes=[pltpu.SemaphoreType.DMA(())],
         compiler_params=params,
-    )(in_hbm(queries[0]))
+    )(in_hbm(waiting))
     first[0], q = lax.optimization_barrier((first[0], q))
     is_high = lax.axis_index("seq") // 2 // half % 2 == 1
     mixed = jnp.where(is_high, first[0], own)
+    mark = pl.pallas_call(
+        mark_kernel,
+        out_shape=pltpu.VMEM((16, HD), jnp.bfloat16),
+        in_specs=[vmem_spec],
+        out_specs=vmem_spec,
+        compiler_params=params,
+        cost_estimate=pl.CostEstimate(flops=0, bytes_accessed=MARK_BYTES, transcendentals=0),
+    )(resident(mixed))
+    came_up, _ = lax.optimization_barrier((first[0], mark))
 
     def across(step):
         return [(lo + (j - step) % half, lo + half + j) for lo in (0, group) for j in range(half)]
@@ -266,7 +280,7 @@
             continue
         path = [half + j, group, *([group + 1] if j % 2 else []), half + j]
         far.append(
-            send(first[0], [(a, c, b, c) for a, b in zip(path, path[1:]) for c in (0, 1)])
+            send(came_up, [(a, c, b, c) for a, b in zip(path, path[1:]) for c in (0, 1)])
         )
 
     def position(source, core, tokens, valid):
@@ -316,7 +330,7 @@
     )(resident(q), resident(starts), *early)
 
     seen, arrived = {}, []
-    for blocks in (far, cross):
+    for blocks in (cross, far):
         held = []
         for block in blocks:
             if id(block) not in seen:
@@ -324,7 +338,7 @@
                 seen[id(block)] = [resident(tied), resident(swap(tied))]
             held += seen[id(block)]
         arrived.append(held)
-    middle, high = arrived
+    high, middle = arrived
     for reads, rows, bases, late in (
         (lambda pair: pair // half % 2 == 1, tokens, high_bases, high),
         (lambda pair: pair == group, tokens // 2, middle_bases, middle),

time: 34.8 us -> 34.8 us (level)
  transfers between devices with their start and end apart: 9 -> 9, of which waited for: 6 -> 7; matrix products, arithmetic and copies ran while one was open for 3% -> 3% of each run, Pallas kernels for 10% -> 10%
where the time goes in v5:
time: 34.8 us; the launch traced here: 34.3 us
  Pallas kernels  17.3 us (50%)
  waiting for transfers between devices  9.48 us (27%)
  starting transfers between devices  6.56 us (19%)
  other arithmetic  0.63 us (2%)
    pallas_call x2, Pallas kernels, per_device(): pl.pallas_call(functools.partial(late_kernel, reads, rows, early_bases, b...  12.9 us
    ppermute x4, waiting for transfers between devices, send(): return lax.ppermute(block, 'seq', closed(devices, seq_count))  6.89 us
    ppermute x4, starting transfers between devices, send(): return lax.ppermute(block, 'seq', closed(devices, seq_count))  5.98 us
    ppermute x5, waiting for transfers between devices, swap(): lax.ppermute(block, 'seq', [(2 * c + i, 2 * c + 1 - i) for c in range(pai...  2.59 us
    pallas_call x1, Pallas kernels, per_device(): pl.pallas_call(functools.partial(early_kernel, group, half, early_bases),...  2.19 us
    pallas_call x1, Pallas kernels, per_device(): pl.pallas_call(load_kernel, out_shape=pltpu.VMEM((tokens, QH * HD), jnp.b...  1.23 us
    pallas_call x1, Pallas kernels, per_device(): pl.pallas_call(join_kernel, out_shape=pltpu.VMEM((tokens, 2 * KVH * HD),...  1 us
  transfers between devices with their start and end apart: 9, of which 7 were waited for; matrix products, arithmetic and copies ran while one was open for 3% of the time, Pallas kernels for 10%

profile of v5, /device:TPU:16, one launch (start us, length us, event | category | flops | bytes accessed | tf_op | source)
XLA Modules:
  0.0 34.3 jit_solution(3437922477714965832)
XLA Ops:
  0.0 1.0 %shard_map.46.refs_0_.early_0_ = bf16[64,2048]{1,0:T(8,128)(2,1)S(1)} custom-call(bf16[64,1024]{1,0:T(8,128)(2,1)} %bitcast.11, bf16[64,1024]{1,0:T(8,128)(2,1)} %bitcast.12), custom_call_target="tpu_custom_call" | custom-call | tf_op jit(solution)/shard_map/pallas_call | solution.py:214
  1.0 0.1 collective-permute-start.1
  1.1 1.6 %collective-permute-start = (bf16[64,2048]{1,0:T(8,128)(2,1)S(1)}, bf16[64,2048]{1,0:T(8,128)(2,1)S(1)}, u32[]{:S(2)}, u32[]{:S(2)}) collective-permute-start(bf16[64,2048]{1,0:T(8,128)(2,1)S(1)} %shard_map.46.refs_0_.early_0_), channel_id=1, source_target_pairs={{0,4},{1,5},{2,6},{3,7},{4,8},{5,9},{6,2},{7,3},{8,12},{9,13},{10,... | collective-permute-start | bytes 786440 | tf_op jit(solution)/shard_map/ppermute | solution.py:199
  2.7 0.3 reduce-window.9
  3.0 0.1 slice.10
  3.2 0.1 slice_reduce_fusion
  3.3 1.5 %collective-permute-start.5 = (bf16[64,2048]{1,0:T(8,128)(2,1)S(1)}, bf16[64,2048]{1,0:T(8,128)(2,1)S(1)}, u32[]{:S(2)}, u32[]{:S(2)}) collective-permute-start(bf16[64,2048]{1,0:T(8,128)(2,1)S(1)} %shard_map.46.refs_0_.early_0_), channel_id=1, source_target_pairs={{0,2},{1,3},{2,0},{3,1},{4,6},{5,7},{6,8},{7,9},{8,10},{9,11},{10,... | collective-permute-start | bytes 786440 | tf_op jit(solution)/shard_map/ppermute | solution.py:199
  4.8 1.2 %shard_map.47.q = bf16[64,8192]{1,0:T(8,128)(2,1)S(1)} custom-call(bf16[64,8192]{1,0:T(8,128)(2,1)} %bitcast.10), custom_call_target="tpu_custom_call" | custom-call | tf_op jit(solution)/shard_map/pallas_call | solution.py:242
  6.1 3.7 %collective-permute-done.refs_2_.early_2_ = bf16[64,2048]{1,0:T(8,128)(2,1)S(1)} collective-permute-done((bf16[64,2048]{1,0:T(8,128)(2,1)S(1)}, bf16[64,2048]{1,0:T(8,128)(2,1)S(1)}, u32[]{:S(2)}, u32[]{:S(2)}) %collective-permute-start) | collective-permute-done | bytes 262176 | tf_op jit(solution)/shard_map/ppermute | solution.py:199
  9.8 2.6 %collective-permute-start.3 = (bf16[64,2048]{1,0:T(8,128)(2,1)S(1)}, bf16[64,2048]{1,0:T(8,128)(2,1)S(1)}, u32[]{:S(2)}, u32[]{:S(2)}) collective-permute-start(bf16[64,2048]{1,0:T(8,128)(2,1)S(1)} %broadcast_select_fusion), channel_id=1, source_target_pairs={{0,6},{1,7},{2,4},{3,5},{4,0},{5,1},{6,8},{7,9},{8,14},{9,15},{10,... | collective-permute-start | bytes 786440 | tf_op jit(solution)/shard_map/ppermute | solution.py:199
  12.4 0.3 collective-permute-start.2
  12.6 0.5 %collective-permute-start.6 = (bf16[64,2048]{1,0:T(8,128)(2,1)S(1)}, bf16[64,2048]{1,0:T(8,128)(2,1)S(1)}, u32[]{:S(2)}, u32[]{:S(2)}) collective-permute-start(bf16[64,2048]{1,0:T(8,128)(2,1)S(1)} %collective-permute-done.5.refs_4_.early_4_), channel_id=1, source_target_pairs={{0,1},{1,0},{2,3},{3,2},{4,5},{5,4},{6,7},{7,6},{8,9},{9,8},{10,11... | collective-permute-start | bytes 786440 | tf_op jit(solution)/shard_map/ppermute | solution.py:202
  13.2 0.1 add_bitcast_fusion
  13.2 0.2 select_reduce_fusion
  13.4 0.8 %collective-permute-done.4.refs_3_.early_3_ = bf16[64,2048]{1,0:T(8,128)(2,1)S(1)} collective-permute-done((bf16[64,2048]{1,0:T(8,128)(2,1)S(1)}, bf16[64,2048]{1,0:T(8,128)(2,1)S(1)}, u32[]{:S(2)}, u32[]{:S(2)}) %collective-permute-start.4) | collective-permute-done | bytes 262176 | tf_op jit(solution)/shard_map/ppermute | solution.py:202
  14.2 0.4 %collective-permute-done.6.refs_5_.early_5_ = bf16[64,2048]{1,0:T(8,128)(2,1)S(1)} collective-permute-done((bf16[64,2048]{1,0:T(8,128)(2,1)S(1)}, bf16[64,2048]{1,0:T(8,128)(2,1)S(1)}, u32[]{:S(2)}, u32[]{:S(2)}) %collective-permute-start.6) | collective-permute-done | bytes 262176 | tf_op jit(solution)/shard_map/ppermute | solution.py:202
  14.6 0.1 broadcast_in_dim.18.starts
  14.6 2.2 %shard_map.48 = (f32[8,512,256]{2,1,0:T(8,128)S(1)}, bf16[64,8192]{1,0:T(8,128)(2,1)}) custom-call(bf16[64,8192]{1,0:T(8,128)(2,1)S(1)} %shard_map.47.q, s32[64,128]{1,0:T(8,128)S(1)} %broadcast_in_dim.18.starts, bf16[64,2048]{1,0:T(8,128)(2,1)S(1)} %shard_map.46.refs_0_.early_0_, bf16[64,2048]{1,0:T(8,128)(2,1)S(1)} %collective-permute-done.1.refs_1_.early_1_, ...), custom_call_target="tpu_custom_call" | custom-call | flops 1 | bytes 1 | tf_op jit(solution)/shard_map/pallas_call | solution.py:322
  16.8 1.8 %collective-permute-done.3.late_0_.late_2_ = bf16[64,2048]{1,0:T(8,128)(2,1)S(1)} collective-permute-done((bf16[64,2048]{1,0:T(8,128)(2,1)S(1)}, bf16[64,2048]{1,0:T(8,128)(2,1)S(1)}, u32[]{:S(2)}, u32[]{:S(2)}) %collective-permute-start.3) | collective-permute-done | bytes 262176 | tf_op jit(solution)/shard_map/ppermute | solution.py:199
  18.7 1.3 %collective-permute-done.2.late_0_ = bf16[64,2048]{1,0:T(8,128)(2,1)S(1)} collective-permute-done((bf16[64,2048]{1,0:T(8,128)(2,1)S(1)}, bf16[64,2048]{1,0:T(8,128)(2,1)S(1)}, u32[]{:S(2)}, u32[]{:S(2)}) %collective-permute-start.2) | collective-permute-done | bytes 262176 | tf_op jit(solution)/shard_map/ppermute | solution.py:199
  20.0 0.2 collective-permute-done.8.late_1_.late_3_
  20.2 0.1 shard_map.49._
  20.3 1.2 %collective-permute-done.7.late_1_ = bf16[64,2048]{1,0:T(8,128)(2,1)S(1)} collective-permute-done((bf16[64,2048]{1,0:T(8,128)(2,1)S(1)}, bf16[64,2048]{1,0:T(8,128)(2,1)S(1)}, u32[]{:S(2)}, u32[]{:S(2)}) %collective-permute-start.7) | collective-permute-done | bytes 262176 | tf_op jit(solution)/shard_map/ppermute | solution.py:202
  21.5 12.8 %shard_map.50 = bf16[64,8192]{1,0:T(8,128)(2,1)} custom-call(bf16[64,8192]{1,0:T(8,128)(2,1)S(1)} %shard_map.47.q, s32[64,128]{1,0:T(8,128)S(1)} %broadcast_in_dim.18.starts, f32[8,512,256]{2,1,0:T(8,128)S(1)} %get-tuple-element.21.summed, bf16[64,2048]{1,0:T(8,128)(2,1)S(1)} %shard_map.46.refs_0_.early_0_, ...), custom_call_target="tpu_custom_call", output_to_operand_aliasing={{}: (13, {})} | custom-call | flops 1 | bytes 1 | tf_op jit(solution)/shard_map/pallas_call | solution.py:346
  (12 shorter events, 0.1 us)
Async XLA Ops:
  0.0 2.7 %copy-start = (s32[2,129]{1,0:T(2,128)S(1)}, s32[2,129]{1,0:T(2,128)}, u32[]{:S(2)}) copy-start(s32[2,129]{1,0:T(2,128)} %param.7) | copy-start | bytes 3100
  1.0 2.3 %collective-permute-start.1 = (bf16[64,2048]{1,0:T(8,128)(2,1)S(1)}, bf16[64,2048]{1,0:T(8,128)(2,1)S(1)}, u32[]{:S(2)}, u32[]{:S(2)}) collective-permute-start(bf16[64,2048]{1,0:T(8,128)(2,1)S(1)} %shard_map.46.refs_0_.early_0_), channel_id=1, source_target_pairs={{0,1},{1,0},{2,3},{3,2},{4,5},{5,4},{6,7},{7,6},{8,9},{9,8},{10,11... | collective-permute-start | bytes 786440 | tf_op jit(solution)/shard_map/ppermute | solution.py:202
  1.1 8.7 %collective-permute-start = (bf16[64,2048]{1,0:T(8,128)(2,1)S(1)}, bf16[64,2048]{1,0:T(8,128)(2,1)S(1)}, u32[]{:S(2)}, u32[]{:S(2)}) collective-permute-start(bf16[64,2048]{1,0:T(8,128)(2,1)S(1)} %shard_map.46.refs_0_.early_0_), channel_id=1, source_target_pairs={{0,4},{1,5},{2,6},{3,7},{4,8},{5,9},{6,2},{7,3},{8,12},{9,13},{10,... | collective-permute-start | bytes 786440 | tf_op jit(solution)/shard_map/ppermute | solution.py:199
  3.3 9.4 %collective-permute-start.5 = (bf16[64,2048]{1,0:T(8,128)(2,1)S(1)}, bf16[64,2048]{1,0:T(8,128)(2,1)S(1)}, u32[]{:S(2)}, u32[]{:S(2)}) collective-permute-start(bf16[64,2048]{1,0:T(8,128)(2,1)S(1)} %shard_map.46.refs_0_.early_0_), channel_id=1, source_target_pairs={{0,2},{1,3},{2,0},{3,1},{4,6},{5,7},{6,8},{7,9},{8,10},{9,11},{10,... | collective-permute-start | bytes 786440 | tf_op jit(solution)/shard_map/ppermute | solution.py:199
  9.8 8.8 %collective-permute-start.3 = (bf16[64,2048]{1,0:T(8,128)(2,1)S(1)}, bf16[64,2048]{1,0:T(8,128)(2,1)S(1)}, u32[]{:S(2)}, u32[]{:S(2)}) collective-permute-start(bf16[64,2048]{1,0:T(8,128)(2,1)S(1)} %broadcast_select_fusion), channel_id=1, source_target_pairs={{0,6},{1,7},{2,4},{3,5},{4,0},{5,1},{6,8},{7,9},{8,14},{9,15},{10,... | collective-permute-start | bytes 786440 | tf_op jit(solution)/shard_map/ppermute | solution.py:199
  12.4 7.6 %collective-permute-start.2 = (bf16[64,2048]{1,0:T(8,128)(2,1)S(1)}, bf16[64,2048]{1,0:T(8,128)(2,1)S(1)}, u32[]{:S(2)}, u32[]{:S(2)}) collective-permute-start(bf16[64,2048]{1,0:T(8,128)(2,1)S(1)} %collective-permute-done.refs_2_.early_2_), channel_id=1, source_target_pairs={{0,1},{1,0},{2,3},{3,2},{4,8},{5,9},{6,7},{7,6},{8,4},{9,5},{10,11... | collective-permute-start | bytes 786440 | tf_op jit(solution)/shard_map/ppermute | solution.py:199
  12.6 1.5 %collective-permute-start.4 = (bf16[64,2048]{1,0:T(8,128)(2,1)S(1)}, bf16[64,2048]{1,0:T(8,128)(2,1)S(1)}, u32[]{:S(2)}, u32[]{:S(2)}) collective-permute-start(bf16[64,2048]{1,0:T(8,128)(2,1)S(1)} %collective-permute-done.refs_2_.early_2_), channel_id=1, source_target_pairs={{0,1},{1,0},{2,3},{3,2},{4,5},{5,4},{6,7},{7,6},{8,9},{9,8},{10,11... | collective-permute-start | bytes 786440 | tf_op jit(solution)/shard_map/ppermute | solution.py:202
  12.6 1.9 %collective-permute-start.6 = (bf16[64,2048]{1,0:T(8,128)(2,1)S(1)}, bf16[64,2048]{1,0:T(8,128)(2,1)S(1)}, u32[]{:S(2)}, u32[]{:S(2)}) collective-permute-start(bf16[64,2048]{1,0:T(8,128)(2,1)S(1)} %collective-permute-done.5.refs_4_.early_4_), channel_id=1, source_target_pairs={{0,1},{1,0},{2,3},{3,2},{4,5},{5,4},{6,7},{7,6},{8,9},{9,8},{10,11... | collective-permute-start | bytes 786440 | tf_op jit(solution)/shard_map/ppermute | solution.py:202
  18.6 1.5 %collective-permute-start.8 = (bf16[64,2048]{1,0:T(8,128)(2,1)S(1)}, bf16[64,2048]{1,0:T(8,128)(2,1)S(1)}, u32[]{:S(2)}, u32[]{:S(2)}) collective-permute-start(bf16[64,2048]{1,0:T(8,128)(2,1)S(1)} %collective-permute-done.3.late_0_.late_2_), channel_id=1, source_target_pairs={{0,1},{1,0},{2,3},{3,2},{4,5},{5,4},{6,7},{7,6},{8,9},{9,8},{10,11... | collective-permute-start | bytes 786440 | tf_op jit(solution)/shard_map/ppermute | solution.py:202
  20.0 1.5 %collective-permute-start.7 = (bf16[64,2048]{1,0:T(8,128)(2,1)S(1)}, bf16[64,2048]{1,0:T(8,128)(2,1)S(1)}, u32[]{:S(2)}, u32[]{:S(2)}) collective-permute-start(bf16[64,2048]{1,0:T(8,128)(2,1)S(1)} %collective-permute-done.2.late_0_), channel_id=1, source_target_pairs={{0,1},{1,0},{2,3},{3,2},{4,5},{5,4},{6,7},{7,6},{8,9},{9,8},{10,11... | collective-permute-start | bytes 786440 | tf_op jit(solution)/shard_map/ppermute | solution.py:202

commit v6 on v5

--- a/solution.py
+++ b/solution.py
@@ -21,10 +21,14 @@
 
 
 def join_kernel(keys, values, joined, sems):
-    copies = [
-        pltpu.make_async_copy(keys, joined.at[:, : KVH * HD], sems.at[0]),
-        pltpu.make_async_copy(values, joined.at[:, KVH * HD :], sems.at[1]),
-    ]
+    parts = sems.shape[0]
+    rows = keys.shape[0] // parts
+    copies = []
+    for part in range(parts):
+        span = slice(part * rows, (part + 1) * rows)
+        for side, source in enumerate((keys, values)):
+            target = joined.at[span, side * KVH * HD : (side + 1) * KVH * HD]
+            copies.append(pltpu.make_async_copy(source.at[span], target, sems.at[part, side]))
     for copy in copies:
         copy.start()
     for copy in copies:
@@ -216,7 +220,7 @@
         out_shape=pltpu.VMEM((tokens, 2 * KVH * HD), jnp.bfloat16),
         in_specs=[any_spec] * 2,
         out_specs=vmem_spec,
-        scratch_shapes=[pltpu.SemaphoreType.DMA((2,))],
+        scratch_shapes=[pltpu.SemaphoreType.DMA((tokens // 16, 2))],
         compiler_params=params,
     )(in_hbm(keys[0]), in_hbm(values[0]))
 

time: 34.8 us -> 34.7 us (level)
  no operation moved by 1% of the time
where the time goes in v6:
time: 34.7 us; the launch traced here: 34.3 us
  Pallas kernels  17.3 us (50%)
  waiting for transfers between devices  9.48 us (27%)
  starting transfers between devices  6.56 us (19%)
  other arithmetic  0.63 us (2%)
    pallas_call x2, Pallas kernels, per_device(): pl.pallas_call(functools.partial(late_kernel, reads, rows, early_bases, b...  12.9 us
    ppermute x4, waiting for transfers between devices, send(): return lax.ppermute(block, 'seq', closed(devices, seq_count))  6.89 us
    ppermute x4, starting transfers between devices, send(): return lax.ppermute(block, 'seq', closed(devices, seq_count))  5.98 us
    ppermute x5, waiting for transfers between devices, swap(): lax.ppermute(block, 'seq', [(2 * c + i, 2 * c + 1 - i) for c in range(pai...  2.59 us
    pallas_call x1, Pallas kernels, per_device(): pl.pallas_call(functools.partial(early_kernel, group, half, early_bases),...  2.19 us
    pallas_call x1, Pallas kernels, per_device(): pl.pallas_call(load_kernel, out_shape=pltpu.VMEM((tokens, QH * HD), jnp.b...  1.23 us
    pallas_call x1, Pallas kernels, per_device(): pl.pallas_call(join_kernel, out_shape=pltpu.VMEM((tokens, 2 * KVH * HD),...  0.95 us
  transfers between devices with their start and end apart: 9, of which 7 were waited for; matrix products, arithmetic and copies ran while one was open for 3% of the time, Pallas kernels for 10%

profile of v6, /device:TPU:16, one launch (start us, length us, event | category | flops | bytes accessed | tf_op | source)
XLA Modules:
  0.0 34.3 jit_solution(12148895643802649890)
XLA Ops:
  0.0 1.0 %shard_map.46.refs_0_.early_0_ = bf16[64,2048]{1,0:T(8,128)(2,1)S(1)} custom-call(bf16[64,1024]{1,0:T(8,128)(2,1)} %bitcast.11, bf16[64,1024]{1,0:T(8,128)(2,1)} %bitcast.12), custom_call_target="tpu_custom_call" | custom-call | tf_op jit(solution)/shard_map/pallas_call | solution.py:218
  1.0 0.1 collective-permute-start.1
  1.0 1.6 %collective-permute-start = (bf16[64,2048]{1,0:T(8,128)(2,1)S(1)}, bf16[64,2048]{1,0:T(8,128)(2,1)S(1)}, u32[]{:S(2)}, u32[]{:S(2)}) collective-permute-start(bf16[64,2048]{1,0:T(8,128)(2,1)S(1)} %shard_map.46.refs_0_.early_0_), channel_id=1, source_target_pairs={{0,4},{1,5},{2,6},{3,7},{4,8},{5,9},{6,2},{7,3},{8,12},{9,13},{10,... | collective-permute-start | bytes 786440 | tf_op jit(solution)/shard_map/ppermute | solution.py:203
  2.7 0.3 reduce-window.9
  3.0 0.1 slice.10
  3.1 0.1 slice_reduce_fusion
  3.2 1.5 %collective-permute-start.5 = (bf16[64,2048]{1,0:T(8,128)(2,1)S(1)}, bf16[64,2048]{1,0:T(8,128)(2,1)S(1)}, u32[]{:S(2)}, u32[]{:S(2)}) collective-permute-start(bf16[64,2048]{1,0:T(8,128)(2,1)S(1)} %shard_map.46.refs_0_.early_0_), channel_id=1, source_target_pairs={{0,2},{1,3},{2,0},{3,1},{4,6},{5,7},{6,8},{7,9},{8,10},{9,11},{10,... | collective-permute-start | bytes 786440 | tf_op jit(solution)/shard_map/ppermute | solution.py:203
  4.8 1.2 %shard_map.47.q = bf16[64,8192]{1,0:T(8,128)(2,1)S(1)} custom-call(bf16[64,8192]{1,0:T(8,128)(2,1)} %bitcast.10), custom_call_target="tpu_custom_call" | custom-call | tf_op jit(solution)/shard_map/pallas_call | solution.py:246
  6.0 3.7 %collective-permute-done.refs_2_.early_2_ = bf16[64,2048]{1,0:T(8,128)(2,1)S(1)} collective-permute-done((bf16[64,2048]{1,0:T(8,128)(2,1)S(1)}, bf16[64,2048]{1,0:T(8,128)(2,1)S(1)}, u32[]{:S(2)}, u32[]{:S(2)}) %collective-permute-start) | collective-permute-done | bytes 262176 | tf_op jit(solution)/shard_map/ppermute | solution.py:203
  9.8 2.6 %collective-permute-start.3 = (bf16[64,2048]{1,0:T(8,128)(2,1)S(1)}, bf16[64,2048]{1,0:T(8,128)(2,1)S(1)}, u32[]{:S(2)}, u32[]{:S(2)}) collective-permute-start(bf16[64,2048]{1,0:T(8,128)(2,1)S(1)} %broadcast_select_fusion), channel_id=1, source_target_pairs={{0,6},{1,7},{2,4},{3,5},{4,0},{5,1},{6,8},{7,9},{8,14},{9,15},{10,... | collective-permute-start | bytes 786440 | tf_op jit(solution)/shard_map/ppermute | solution.py:203
  12.3 0.3 collective-permute-start.2
  12.6 0.5 %collective-permute-start.6 = (bf16[64,2048]{1,0:T(8,128)(2,1)S(1)}, bf16[64,2048]{1,0:T(8,128)(2,1)S(1)}, u32[]{:S(2)}, u32[]{:S(2)}) collective-permute-start(bf16[64,2048]{1,0:T(8,128)(2,1)S(1)} %collective-permute-done.5.refs_4_.early_4_), channel_id=1, source_target_pairs={{0,1},{1,0},{2,3},{3,2},{4,5},{5,4},{6,7},{7,6},{8,9},{9,8},{10,11... | collective-permute-start | bytes 786440 | tf_op jit(solution)/shard_map/ppermute | solution.py:206
  13.1 0.1 add_bitcast_fusion
  13.2 0.2 select_reduce_fusion
  13.4 0.8 %collective-permute-done.4.refs_3_.early_3_ = bf16[64,2048]{1,0:T(8,128)(2,1)S(1)} collective-permute-done((bf16[64,2048]{1,0:T(8,128)(2,1)S(1)}, bf16[64,2048]{1,0:T(8,128)(2,1)S(1)}, u32[]{:S(2)}, u32[]{:S(2)}) %collective-permute-start.4) | collective-permute-done | bytes 262176 | tf_op jit(solution)/shard_map/ppermute | solution.py:206
  14.1 0.4 %collective-permute-done.6.refs_5_.early_5_ = bf16[64,2048]{1,0:T(8,128)(2,1)S(1)} collective-permute-done((bf16[64,2048]{1,0:T(8,128)(2,1)S(1)}, bf16[64,2048]{1,0:T(8,128)(2,1)S(1)}, u32[]{:S(2)}, u32[]{:S(2)}) %collective-permute-start.6) | collective-permute-done | bytes 262176 | tf_op jit(solution)/shard_map/ppermute | solution.py:206
  14.5 0.1 broadcast_in_dim.18.starts
  14.6 2.2 %shard_map.48 = (f32[8,512,256]{2,1,0:T(8,128)S(1)}, bf16[64,8192]{1,0:T(8,128)(2,1)}) custom-call(bf16[64,8192]{1,0:T(8,128)(2,1)S(1)} %shard_map.47.q, s32[64,128]{1,0:T(8,128)S(1)} %broadcast_in_dim.18.starts, bf16[64,2048]{1,0:T(8,128)(2,1)S(1)} %shard_map.46.refs_0_.early_0_, bf16[64,2048]{1,0:T(8,128)(2,1)S(1)} %collective-permute-done.1.refs_1_.early_1_, ...), custom_call_target="tpu_custom_call" | custom-call | flops 1 | bytes 1 | tf_op jit(solution)/shard_map/pallas_call | solution.py:326
  16.8 1.8 %collective-permute-done.3.late_0_.late_2_ = bf16[64,2048]{1,0:T(8,128)(2,1)S(1)} collective-permute-done((bf16[64,2048]{1,0:T(8,128)(2,1)S(1)}, bf16[64,2048]{1,0:T(8,128)(2,1)S(1)}, u32[]{:S(2)}, u32[]{:S(2)}) %collective-permute-start.3) | collective-permute-done | bytes 262176 | tf_op jit(solution)/shard_map/ppermute | solution.py:203
  18.6 1.3 %collective-permute-done.2.late_0_ = bf16[64,2048]{1,0:T(8,128)(2,1)S(1)} collective-permute-done((bf16[64,2048]{1,0:T(8,128)(2,1)S(1)}, bf16[64,2048]{1,0:T(8,128)(2,1)S(1)}, u32[]{:S(2)}, u32[]{:S(2)}) %collective-permute-start.2) | collective-permute-done | bytes 262176 | tf_op jit(solution)/shard_map/ppermute | solution.py:203
  19.9 0.2 collective-permute-done.8.late_1_.late_3_
  20.1 0.1 shard_map.49._
  20.2 1.2 %collective-permute-done.7.late_1_ = bf16[64,2048]{1,0:T(8,128)(2,1)S(1)} collective-permute-done((bf16[64,2048]{1,0:T(8,128)(2,1)S(1)}, bf16[64,2048]{1,0:T(8,128)(2,1)S(1)}, u32[]{:S(2)}, u32[]{:S(2)}) %collective-permute-start.7) | collective-permute-done | bytes 262176 | tf_op jit(solution)/shard_map/ppermute | solution.py:206
  21.5 12.8 %shard_map.50 = bf16[64,8192]{1,0:T(8,128)(2,1)} custom-call(bf16[64,8192]{1,0:T(8,128)(2,1)S(1)} %shard_map.47.q, s32[64,128]{1,0:T(8,128)S(1)} %broadcast_in_dim.18.starts, f32[8,512,256]{2,1,0:T(8,128)S(1)} %get-tuple-element.21.summed, bf16[64,2048]{1,0:T(8,128)(2,1)S(1)} %shard_map.46.refs_0_.early_0_, ...), custom_call_target="tpu_custom_call", output_to_operand_aliasing={{}: (13, {})} | custom-call | flops 1 | bytes 1 | tf_op jit(solution)/shard_map/pallas_call | solution.py:350
  (12 shorter events, 0.1 us)
Async XLA Ops:
  0.0 2.7 %copy-start = (s32[2,129]{1,0:T(2,128)S(1)}, s32[2,129]{1,0:T(2,128)}, u32[]{:S(2)}) copy-start(s32[2,129]{1,0:T(2,128)} %param.7) | copy-start | bytes 3100
  1.0 2.3 %collective-permute-start.1 = (bf16[64,2048]{1,0:T(8,128)(2,1)S(1)}, bf16[64,2048]{1,0:T(8,128)(2,1)S(1)}, u32[]{:S(2)}, u32[]{:S(2)}) collective-permute-start(bf16[64,2048]{1,0:T(8,128)(2,1)S(1)} %shard_map.46.refs_0_.early_0_), channel_id=1, source_target_pairs={{0,1},{1,0},{2,3},{3,2},{4,5},{5,4},{6,7},{7,6},{8,9},{9,8},{10,11... | collective-permute-start | bytes 786440 | tf_op jit(solution)/shard_map/ppermute | solution.py:206
  1.0 8.7 %collective-permute-start = (bf16[64,2048]{1,0:T(8,128)(2,1)S(1)}, bf16[64,2048]{1,0:T(8,128)(2,1)S(1)}, u32[]{:S(2)}, u32[]{:S(2)}) collective-permute-start(bf16[64,2048]{1,0:T(8,128)(2,1)S(1)} %shard_map.46.refs_0_.early_0_), channel_id=1, source_target_pairs={{0,4},{1,5},{2,6},{3,7},{4,8},{5,9},{6,2},{7,3},{8,12},{9,13},{10,... | collective-permute-start | bytes 786440 | tf_op jit(solution)/shard_map/ppermute | solution.py:203
  3.2 9.4 %collective-permute-start.5 = (bf16[64,2048]{1,0:T(8,128)(2,1)S(1)}, bf16[64,2048]{1,0:T(8,128)(2,1)S(1)}, u32[]{:S(2)}, u32[]{:S(2)}) collective-permute-start(bf16[64,2048]{1,0:T(8,128)(2,1)S(1)} %shard_map.46.refs_0_.early_0_), channel_id=1, source_target_pairs={{0,2},{1,3},{2,0},{3,1},{4,6},{5,7},{6,8},{7,9},{8,10},{9,11},{10,... | collective-permute-start | bytes 786440 | tf_op jit(solution)/shard_map/ppermute | solution.py:203
  9.8 8.8 %collective-permute-start.3 = (bf16[64,2048]{1,0:T(8,128)(2,1)S(1)}, bf16[64,2048]{1,0:T(8,128)(2,1)S(1)}, u32[]{:S(2)}, u32[]{:S(2)}) collective-permute-start(bf16[64,2048]{1,0:T(8,128)(2,1)S(1)} %broadcast_select_fusion), channel_id=1, source_target_pairs={{0,6},{1,7},{2,4},{3,5},{4,0},{5,1},{6,8},{7,9},{8,14},{9,15},{10,... | collective-permute-start | bytes 786440 | tf_op jit(solution)/shard_map/ppermute | solution.py:203
  12.3 7.6 %collective-permute-start.2 = (bf16[64,2048]{1,0:T(8,128)(2,1)S(1)}, bf16[64,2048]{1,0:T(8,128)(2,1)S(1)}, u32[]{:S(2)}, u32[]{:S(2)}) collective-permute-start(bf16[64,2048]{1,0:T(8,128)(2,1)S(1)} %collective-permute-done.refs_2_.early_2_), channel_id=1, source_target_pairs={{0,1},{1,0},{2,3},{3,2},{4,8},{5,9},{6,7},{7,6},{8,4},{9,5},{10,11... | collective-permute-start | bytes 786440 | tf_op jit(solution)/shard_map/ppermute | solution.py:203
  12.6 1.5 %collective-permute-start.4 = (bf16[64,2048]{1,0:T(8,128)(2,1)S(1)}, bf16[64,2048]{1,0:T(8,128)(2,1)S(1)}, u32[]{:S(2)}, u32[]{:S(2)}) collective-permute-start(bf16[64,2048]{1,0:T(8,128)(2,1)S(1)} %collective-permute-done.refs_2_.early_2_), channel_id=1, source_target_pairs={{0,1},{1,0},{2,3},{3,2},{4,5},{5,4},{6,7},{7,6},{8,9},{9,8},{10,11... | collective-permute-start | bytes 786440 | tf_op jit(solution)/shard_map/ppermute | solution.py:206
  12.6 1.9 %collective-permute-start.6 = (bf16[64,2048]{1,0:T(8,128)(2,1)S(1)}, bf16[64,2048]{1,0:T(8,128)(2,1)S(1)}, u32[]{:S(2)}, u32[]{:S(2)}) collective-permute-start(bf16[64,2048]{1,0:T(8,128)(2,1)S(1)} %collective-permute-done.5.refs_4_.early_4_), channel_id=1, source_target_pairs={{0,1},{1,0},{2,3},{3,2},{4,5},{5,4},{6,7},{7,6},{8,9},{9,8},{10,11... | collective-permute-start | bytes 786440 | tf_op jit(solution)/shard_map/ppermute | solution.py:206
  18.6 1.5 %collective-permute-start.8 = (bf16[64,2048]{1,0:T(8,128)(2,1)S(1)}, bf16[64,2048]{1,0:T(8,128)(2,1)S(1)}, u32[]{:S(2)}, u32[]{:S(2)}) collective-permute-start(bf16[64,2048]{1,0:T(8,128)(2,1)S(1)} %collective-permute-done.3.late_0_.late_2_), channel_id=1, source_target_pairs={{0,1},{1,0},{2,3},{3,2},{4,5},{5,4},{6,7},{7,6},{8,9},{9,8},{10,11... | collective-permute-start | bytes 786440 | tf_op jit(solution)/shard_map/ppermute | solution.py:206
  19.9 1.5 %collective-permute-start.7 = (bf16[64,2048]{1,0:T(8,128)(2,1)S(1)}, bf16[64,2048]{1,0:T(8,128)(2,1)S(1)}, u32[]{:S(2)}, u32[]{:S(2)}) collective-permute-start(bf16[64,2048]{1,0:T(8,128)(2,1)S(1)} %collective-permute-done.2.late_0_), channel_id=1, source_target_pairs={{0,1},{1,0},{2,3},{3,2},{4,5},{5,4},{6,7},{7,6},{8,9},{9,8},{10,11... | collective-permute-start | bytes 786440 | tf_op jit(solution)/shard_map/ppermute | solution.py:206
